TPU v7x, 256 devices: a whole 4x4x8 slice. The times are simulated.
256 devices in a mesh: ctx: 16 (over y, z_lo), head: 8 (over x, core), grp: 2 (over z_hi).
Axes of the slice: x: 4, y: 4, z: 8 (z_hi: 2, z_lo: 4; z = z_hi * 4 + z_lo), core: 2. Of those that a mesh axis runs over, the one named last changes fastest.
Arguments:
- span_q: bfloat16 [2, 2048, 8192], P('grp', 'ctx', 'head'), may hold values from -6 to 6
- span_kv: bfloat16 [2, 2, 2048, 1024], P('grp', None, 'ctx', 'head'), may hold values from -6 to 6
- prefix_kv: bfloat16 [2, 2, 14336, 1024], P('grp', None, 'ctx', 'head'), may hold values from -6 to 6
- prefix_len: int32 [2], P('grp'), may hold values from 7168 to 14336, as said below
- dec_q: bfloat16 [2, 256, 4, 8192], P('grp', 'ctx', None, 'head'), may hold values from -6 to 6
- dec_new_kv: bfloat16 [2, 2, 256, 4, 1024], P('grp', None, 'ctx', None, 'head'), may hold values from -6 to 6
- dec_cache: bfloat16 [2, 2, 256, 512, 1024], P('grp', None, 'ctx', None, 'head'), may hold values from -6 to 6
- cache_len: int32 [2, 256], P('grp', 'ctx'), may hold values from 32 to 512, as said below
- prompt_row: int32 [2], P('grp'), may hold values from 0 to 255
- out_weight: bfloat16 [8192, 8192], P('head', 'ctx'), may hold values from -0.0625 to 0.0625
Outputs:
- prefill_out: bfloat16 [2, 2048, 8192], P('grp', 'ctx', 'head')
- decode_out: bfloat16 [2, 256, 4, 8192], P('grp', 'head', None, 'ctx')
Inputs may be any that keep to these rules, and one draw needn't show every extreme that they name: `prefix_len`: some group uses all 14336 prefix slots. `cache_len`: some row of each group uses all 512 slots.
All inputs are finite; a program needn't handle non-finite values.
Results may differ from a plain program's by a relative error of at most 0.019.
Values may be sent and summed in bfloat16 or wider, within the bound.
A program may use at most 192 MiB of HBM per device.

v0:
```python
import math

import jax
import jax.numpy as jnp
from jax import lax
from jax.sharding import PartitionSpec as P

HD = 128
GQ = 8


MASKED_SCORE = -1e30


def swapped(block, axis, stride):
    count = lax.axis_size(axis)
    route = []
    for low in range(count):
        high = low | 1 << stride
        if high != low and high < count:
            route += [(low, high), (high, low)]
    return lax.ppermute(block, axis, route)


def absorb(soft_state, scores, usable, values, einsum_form):
    row_max, row_total, weighted = soft_state
    masked = jnp.where(usable, scores, MASKED_SCORE)
    new_max = jnp.maximum(row_max, jnp.max(masked, axis=-1))
    weights = jnp.where(usable, jnp.exp(masked - new_max[..., None]), 0.0)
    rescale = jnp.exp(row_max - new_max)
    row_total = row_total * rescale + jnp.sum(weights, axis=-1)
    weighted = weighted * rescale[..., None] + jnp.einsum(
        einsum_form, weights.astype(jnp.bfloat16), values, preferred_element_type=jnp.float32
    )
    return (new_max, row_total, weighted)


def empty_state(lead_shape):
    return (
        jnp.full(lead_shape, MASKED_SCORE, jnp.float32),
        jnp.zeros(lead_shape, jnp.float32),
        jnp.zeros(lead_shape + (HD,), jnp.float32),
    )


def combine(first_state, second_state):
    new_max = jnp.maximum(first_state[0], second_state[0])
    first_scale = jnp.exp(first_state[0] - new_max)
    second_scale = jnp.exp(second_state[0] - new_max)
    return (
        new_max,
        first_state[1] * first_scale + second_state[1] * second_scale,
        first_state[2] * first_scale[..., None] + second_state[2] * second_scale[..., None],
    )


def finish(soft_state):
    return (soft_state[2] / soft_state[1][..., None]).astype(jnp.bfloat16)


def shards(
    span_q,
    span_kv,
    prefix_kv,
    prefix_len,
    dec_q,
    dec_new_kv,
    dec_cache,
    cache_len,
    prompt_row,
    out_weight,
):
    score_scale = 1.0 / math.sqrt(HD)
    span_rows = span_q.shape[1]
    prefix_rows = prefix_kv.shape[2]
    local_heads = span_kv.shape[-1] // HD
    my_index = lax.axis_index("ctx")
    queries = span_q[0].reshape(span_rows, local_heads, GQ, HD)
    prefix_valid = prefix_len[0]
    query_pos = my_index * span_rows + jnp.arange(span_rows, dtype=jnp.int32)
    start_state = empty_state((span_rows, local_heads, GQ))
    block_len = prefix_rows + span_rows
    local_kv = jnp.concatenate([prefix_kv[0], span_kv[0]], axis=1)
    shard_piece = lax.all_gather(local_kv, "ctx", axis=1, tiled=True)
    piece_rows = shard_piece.shape[1] // block_len
    shaped = shard_piece.reshape(2, piece_rows * block_len, local_heads, HD)
    within = jnp.arange(block_len, dtype=jnp.int32)[None, :]
    shard_ids = jnp.arange(piece_rows, dtype=jnp.int32)[:, None]
    prefix_ok = shard_ids * prefix_rows + within < prefix_valid
    span_ok = (shard_ids * span_rows + within - prefix_rows)[None] <= query_pos[:, None, None]
    usable = jnp.where((within < prefix_rows)[None], prefix_ok[None], span_ok)
    usable = usable.reshape(span_rows, 1, 1, piece_rows * block_len)
    scores = (
        jnp.einsum("tkgd,lkd->tkgl", queries, shaped[0], preferred_element_type=jnp.float32)
        * score_scale
    )
    soft_state = absorb(start_state, scores, usable, shaped[1], "tkgl,lkd->tkgd")
    prefill_out = finish(soft_state).reshape(1, span_rows, local_heads * GQ * HD)
    arrived = swapped(span_kv, "grp", 0)
    row_count = dec_q.shape[1]
    step_count = dec_q.shape[2]
    slot_count = dec_cache.shape[3]
    dec_queries = dec_q[0].reshape(row_count, step_count, local_heads, GQ, HD)
    cache_rows = dec_cache[0].reshape(2, row_count, slot_count, local_heads, HD)
    cache_scores = (
        jnp.einsum(
            "rskgd,rlkd->rskgl", dec_queries, cache_rows[0], preferred_element_type=jnp.float32
        )
        * score_scale
    )
    cache_ok = (jnp.arange(slot_count, dtype=jnp.int32)[None, :] < cache_len[0][:, None])[
        :, None, None, None, :
    ]
    lead_shape = (row_count, step_count, local_heads, GQ)
    row_state = absorb(
        empty_state(lead_shape), cache_scores, cache_ok, cache_rows[1], "rskgl,rlkd->rskgd"
    )
    new_rows = dec_new_kv[0].reshape(2, row_count, step_count, local_heads, HD)
    new_scores = (
        jnp.einsum(
            "rskgd,rlkd->rskgl", dec_queries, new_rows[0], preferred_element_type=jnp.float32
        )
        * score_scale
    )
    step_ids = jnp.arange(step_count, dtype=jnp.int32)
    new_ok = (step_ids[None, :] <= step_ids[:, None])[None, :, None, None, :]
    row_state = absorb(row_state, new_scores, new_ok, new_rows[1], "rskgl,rlkd->rskgd")
    prompt_index = prompt_row[0]
    row_ids = my_index * row_count + jnp.arange(row_count, dtype=jnp.int32)
    is_prompt = row_ids == prompt_index
    local_row = jnp.clip(prompt_index - my_index * row_count, 0, row_count - 1)
    picked = lax.dynamic_index_in_dim(dec_queries, local_row, 0, keepdims=False)
    all_usable = jnp.ones((1, 1, 1, 1), dtype=jnp.bool_)
    full_span = lax.all_gather(arrived, "ctx", axis=2, tiled=True)
    moved = full_span[0].reshape(2, full_span.shape[2], local_heads, HD)
    moved_scores = (
        jnp.einsum("skgd,lkd->skgl", picked, moved[0], preferred_element_type=jnp.float32)
        * score_scale
    )
    merged = absorb(
        empty_state((step_count, local_heads, GQ)),
        moved_scores,
        all_usable,
        moved[1],
        "skgl,lkd->skgd",
    )
    selector = is_prompt[:, None, None, None]
    extra_state = (
        jnp.where(selector, merged[0][None], MASKED_SCORE),
        jnp.where(selector, merged[1][None], 0.0),
        jnp.where(selector[..., None], merged[2][None], 0.0),
    )
    row_state = combine(row_state, extra_state)
    attended = finish(row_state).reshape(row_count, step_count, local_heads * GQ * HD)
    shard_piece = lax.all_gather(attended, "ctx", axis=0, tiled=True)
    piece_rows = shard_piece.shape[0]
    flattened = shard_piece.reshape(piece_rows * step_count, shard_piece.shape[2])
    product = jnp.dot(flattened, out_weight, preferred_element_type=jnp.float32)
    partial_terms = product.reshape(piece_rows, step_count, out_weight.shape[1])
    summed = lax.psum_scatter(
        partial_terms.astype(jnp.bfloat16), "head", scatter_dimension=0, tiled=True
    )
    decode_out = summed[None]
    return (prefill_out, decode_out)


def solution(mesh):
    placed = (
        P("grp", "ctx", "head"),
        P("grp", None, "ctx", "head"),
        P("grp", None, "ctx", "head"),
        P("grp"),
        P("grp", "ctx", None, "head"),
        P("grp", None, "ctx", None, "head"),
        P("grp", None, "ctx", None, "head"),
        P("grp", "ctx"),
        P("grp"),
        P("head", "ctx"),
    )
    return jax.shard_map(
        shards,
        mesh=mesh,
        in_specs=placed,
        out_specs=(P("grp", "ctx", "head"), P("grp", "head", None, "ctx")),
        check_vma=False,
    )
```

profile of v0, /device:TPU:16, one launch (start us, length us, event | category | flops | bytes accessed | tf_op | source)
XLA Modules:
  0.0 499.7 jit_solution(14101065672736690138)
XLA Ops:
  7.2 7.3 %collective-permute-start = (bf16[1,2,128,128]{3,2,1,0:T(8,128)(2,1)}, bf16[1,2,128,128]{3,2,1,0:T(8,128)(2,1)S(1)}, u32[]{:S(2)}, u32[]{:S(2)}) collective-permute-start(bf16[1,2,128,128]{3,2,1,0:T(8,128)(2,1)} %param.11), channel_id=1, source_target_pairs={{0,1},{1,0},{2,3},{3,2},{4,5},{5,4},{6,7},{7,6},{8,9},{9,8},{10,11... | collective-permute-start | bytes 196616 | tf_op jit(solution)/shard_map/ppermute | solution.py:22
  14.5 2.7 collective-permute-done
  17.3 0.6 copy-done.4
  18.0 1.0 reshape.454
  18.9 1.0 reshape_squeeze.2
  20.6 0.7 iota_compare_fusion
  21.3 1.4 fusion.99
  22.8 2.5 fusion.98
  25.3 0.2 fusion.72
  25.4 0.4 fusion.59
  25.8 69.8 %all-gather.6.cloned.1.call-done = bf16[1,2,2048,128]{3,2,1,0:T(8,128)(2,1)} async-done(((bf16[1,2,128,128]{3,2,1,0:T(8,128)(2,1)}), bf16[1,2,2048,128]{3,2,1,0:T(8,128)(2,1)}) %all-gather.6.cloned.1.call-update) | async-done | bytes 1048592 | tf_op jit(solution)/shard_map/all_gather | solution.py:134
  95.6 1.4 fusion.100
  97.0 0.2 fusion.67
  97.2 0.1 multiply_add_fusion
  97.4 2.2 fusion.44
  99.6 1.3 fusion.50
  100.9 0.4 fusion.47
  101.4 0.7 copy.16
  102.2 84.9 %all-gather.8.cloned.1.call-done = bf16[256,4,1024]{2,0,1:T(8,128)(2,1)} async-done(((bf16[16,4,1024]{2,0,1:T(8,128)(2,1)}), bf16[256,4,1024]{2,0,1:T(8,128)(2,1)}) %all-gather.8.cloned.1.call-update) | async-done | bytes 2097168 | tf_op jit(solution)/shard_map/all_gather | solution.py:155
  187.0 3.8 convolution_convert_fusion
  190.9 0.2 all-gather.4.cloned.1.call-start
  191.1 0.8 pad_maximum_fusion
  192.8 0.1 add.141
  193.0 0.1 add.146
  193.1 7.8 %compare_select_fusion = pred[128,16384]{0,1:T(8,128)(4,1)S(1)} fusion(s32[128]{0:T(128)S(1)} %iota_add_fusion, s32[16384]{0:T(1024)S(1)} %add_add_fusion, pred[16384]{0:T(1024)(128)(4,1)S(1)} %add_compare_fusion, pred[16384]{0:T(1024)(128)(4,1)S(1)} %bitcast.241), kind=kLoop, calls=%fused_computation.8 | loop fusion | flops 4194304 | bytes 2195968 | tf_op jit(solution)/shard_map/jit(_where)/select_n | solution.py:91
  200.9 31.5 %reduce-scatter.2.cloned.1.call-done = bf16[32,4,512]{2,0,1:T(8,128)(2,1)} async-done(((bf16[256,4,512]{2,0,1:T(8,128)(2,1)}), bf16[32,4,512]{2,0,1:T(8,128)(2,1)}) %reduce-scatter.2.cloned.1.call-update) | async-done | bytes 131088 | tf_op jit(solution)/shard_map/reduce_scatter | solution.py:160
  232.4 1.7 copy.18
  234.1 184.5 %all-gather.4.cloned.1.call-done = bf16[2,16384,128]{2,1,0:T(8,128)(2,1)} async-done(((bf16[2,1024,128]{2,1,0:T(8,128)(2,1)}), bf16[2,16384,128]{2,1,0:T(8,128)(2,1)}) %all-gather.4.cloned.1.call-update) | async-done | bytes 8388624 | tf_op jit(solution)/shard_map/all_gather | solution.py:84
  418.6 26.4 %fusion = (f32[128,8]{0,1:T(8,128)S(1)}, f32[16384,128,8]{1,0,2:T(8,128)}) fusion(pred[128,16384]{0,1:T(8,128)(4,1)S(1)} %compare_select_fusion, bf16[128,8,128]{2,1,0:T(8,128)(2,1)S(1)} %bitcast.236, bf16[2,16384,128]{2,1,0:T(8,128)(2,1)} %all-gather.4.cloned.1.call-done), kind=kOutput, calls=%fused_computation.2 | convolution fusion | flops 4345297920 | bytes 73666560 | tf_op jit(solution)/shard_map/tkgd,lkd->tkgl/dot_general | solution.py:94
  445.0 21.4 %fusion.1 = f32[128,8]{0,1:T(8,128)S(1)} fusion(f32[16384,128,8]{1,0,2:T(8,128)} %get-tuple-element.16, f32[128,8]{0,1:T(8,128)S(1)} %broadcast_maximum_fusion.1, pred[128,16384]{0,1:T(8,128)(4,1)S(1)} %compare_select_fusion), kind=kLoop, calls=%fused_computation.3 | loop fusion | flops 83885056 | bytes 69214208 | tf_op jit(solution)/shard_map/reduce_sum | solution.py:31
  466.4 25.9 %fusion.55 = bf16[1,128,128,8]{2,1,3,0:T(8,128)(2,1)S(1)} fusion(f32[16384,128,8]{1,0,2:T(8,128)} %get-tuple-element.16, f32[128,8]{0,1:T(8,128)S(1)} %broadcast_maximum_fusion.1, pred[128,16384]{0,1:T(8,128)(4,1)S(1)} %compare_select_fusion, bf16[2,16384,128]{2,1,0:T(8,128)(2,1)} %all-gather.4.cloned.1.call-done, f32[128,8]{0,1:T(8,128)S(1)} %get-tuple-element.12, ...), kind=kOutput, calls=%fused_computation.44 | convolution fusion | flops 4379246592 | bytes 73674752 | tf_op jit(solution)/shard_map/tkgl,lkd->tkgd/dot_general | solution.py:32
  492.3 0.9 copy.17
  (37 shorter events, 0.5 us)
Async XLA Ops:
  7.2 179.9 %copy-start = (bf16[1024,512]{1,0:T(8,128)(2,1)S(1)}, bf16[1024,512]{1,0:T(8,128)(2,1)}, u32[]{:S(2)}) copy-start(bf16[1024,512]{1,0:T(8,128)(2,1)} %param.19) | copy-start | bytes 3145732
  7.2 93.7 %copy-start.5 = (bf16[1,2,16,4,128]{4,3,2,1,0:T(4,128)(2,1)S(1)}, bf16[1,2,16,4,128]{4,3,2,1,0:T(4,128)(2,1)}, u32[]{:S(2)}) copy-start(bf16[1,2,16,4,128]{4,3,2,1,0:T(4,128)(2,1)} %param.15) | copy-start | bytes 98308
  7.2 88.4 %all-gather.6.cloned.1.call-start = ((), (), s32[]{:S(2)}) async-start(), calls=%async_computation.2 | async-start | bytes 1114112 | tf_op jit(solution)/shard_map/all_gather | solution.py:134
  7.2 10.0 %collective-permute-start = (bf16[1,2,128,128]{3,2,1,0:T(8,128)(2,1)}, bf16[1,2,128,128]{3,2,1,0:T(8,128)(2,1)S(1)}, u32[]{:S(2)}, u32[]{:S(2)}) collective-permute-start(bf16[1,2,128,128]{3,2,1,0:T(8,128)(2,1)} %param.11), channel_id=1, source_target_pairs={{0,1},{1,0},{2,3},{3,2},{4,5},{5,4},{6,7},{7,6},{8,9},{9,8},{10,11... | collective-permute-start | bytes 196616 | tf_op jit(solution)/shard_map/ppermute | solution.py:22
  17.3 0.6 copy-start.4
  17.9 169.1 %all-gather.8.cloned.1.call-start = ((), (), s32[]{:S(2)}) async-start(), calls=%async_computation.3 | async-start | bytes 2228224 | tf_op jit(solution)/shard_map/all_gather | solution.py:155
  97.3 93.8 %copy-start.1 = (bf16[1,2,896,128]{3,2,1,0:T(8,128)(2,1)S(1)}, bf16[1,2,896,128]{3,2,1,0:T(8,128)(2,1)}, u32[]{:S(2)}) copy-start(bf16[1,2,896,128]{3,2,1,0:T(8,128)(2,1)} %param.12) | copy-start | bytes 1376260
  97.3 93.8 %copy-start.3 = (bf16[1,2,128,128]{3,2,1,0:T(8,128)(2,1)S(1)}, bf16[1,2,128,128]{3,2,1,0:T(8,128)(2,1)}, u32[]{:S(2)}) copy-start(bf16[1,2,128,128]{3,2,1,0:T(8,128)(2,1)} %param.11) | copy-start | bytes 196612
  97.4 95.4 %copy-start.2 = (bf16[1,128,1024]{2,1,0:T(8,128)(2,1)S(1)}, bf16[1,128,1024]{2,1,0:T(8,128)(2,1)}, u32[]{:S(2)}) copy-start(bf16[1,128,1024]{2,1,0:T(8,128)(2,1)} %param.10) | copy-start | bytes 786436
  102.1 130.3 %reduce-scatter.2.cloned.1.call-start = ((), (), s32[]{:S(2)}) async-start(), calls=%async_computation.4 | async-start | bytes 1179648 | tf_op jit(solution)/shard_map/reduce_scatter | solution.py:160
  190.9 227.7 %all-gather.4.cloned.1.call-start = ((), (), s32[]{:S(2)}) async-start(), calls=%async_computation.1 | async-start | bytes 8912896 | tf_op jit(solution)/shard_map/all_gather | solution.py:84
Sparse Core Ops, SparseCore 0:
  18.0 77.5 all-gather.5
  102.2 84.7 all-gather.7
  191.0 41.3 reduce-scatter.1
  234.1 184.4 all-gather.3
where the time goes:
time: 503 us; the launch traced here: 500 us
  waiting for transfers between devices  374 us (74%)
  matrix products  65.4 us (13%)
  other arithmetic  31.8 us (6%)
  between operations  15.3 us (3%)
  starting transfers between devices  7.62 us (2%)
  local copies, waits for them, and re-layouts  6.12 us (1%)
    all_gather x1, waiting for transfers between devices, shards(): shard_piece = lax.all_gather(local_kv, 'ctx', axis=1, tiled=True)  185 us
    all_gather x1, waiting for transfers between devices, shards(): shard_piece = lax.all_gather(attended, 'ctx', axis=0, tiled=True)  84.9 us
    all_gather x1, waiting for transfers between devices, shards(): full_span = lax.all_gather(arrived, 'ctx', axis=2, tiled=True)  69.8 us
    reduce_scatter x1, waiting for transfers between devices, shards(): lax.psum_scatter(partial_terms.astype(jnp.bfloat16), 'head', scatter_dime...  31.5 us
    dot_general x4, matrix products, absorb(): jnp.einsum(einsum_form, weights.astype(jnp.bfloat16), values, preferred_e...  29.9 us
    dot_general x1, matrix products, shards(): jnp.einsum('tkgd,lkd->tkgl', queries, shaped[0], preferred_element_type=j...  26.4 us
    reduce_sum x4, other arithmetic, absorb(): row_total = row_total * rescale + jnp.sum(weights, axis=-1)  22.2 us
  transfers between devices with their start and end apart: 5, of which 5 were waited for; matrix products, arithmetic and copies ran while one was open for 4% of the time, Pallas kernels for 0%

commit v1 on v0

v1 whole, which is shorter than its diff:
```python
import math

import jax
import jax.numpy as jnp
from jax import lax
from jax.experimental import pallas as pl
from jax.experimental.pallas import tpu as pltpu
from jax.sharding import PartitionSpec as P

HD = 128
GQ = 8
RING = 4
PRE = 896
SPAN = 128
KEYS = PRE + SPAN
ROWS = 16
STEPS = 4
SLOTS = 512
QROWS = STEPS * GQ
COLS = 512
MASKED = -1e30
LOG2E = math.log2(math.e)
SCALE = LOG2E / math.sqrt(HD)
MESH = pl.DeviceIdType.MESH
F32 = jnp.float32
BF16 = jnp.bfloat16
BLOCK = 512
VMEM_BYTES = 40 * 1024 * 1024

PIECES = (0, 1, 1, 1, 2, 2, 2, 2, 3, 3, 3, 3, 1, 0, 0, 0)
CHUNKS = (0, 0, 1, 2, 0, 1, 2, 3, 0, 1, 2, 3, 3, 1, 2, 3)


def dot_nt(a, b):
    return lax.dot_general(a, b, (((1,), (1,)), ((), ())), preferred_element_type=F32)


def dot_nn(a, b):
    return lax.dot_general(a, b, (((1,), (0,)), ((), ())), preferred_element_type=F32)


def log2(v):
    return jnp.log(v) * LOG2E


def iota(shape, axis):
    return lax.broadcasted_iota(jnp.int32, shape, axis)


def lookup(table, index):
    value = jnp.int32(table[0])
    for at, entry in enumerate(table[1:], 1):
        value = jnp.where(index == at, jnp.int32(entry), value)
    return value


def to_row(column):
    shape = column.shape
    return jnp.sum(jnp.where(iota(shape, 0) == iota(shape, 1), column, 0.0), axis=0, keepdims=True)


def to_column(row, count):
    shape = (count, HD)
    spread = jnp.broadcast_to(row, shape)
    return jnp.sum(jnp.where(iota(shape, 0) == iota(shape, 1), spread, 0.0), axis=1, keepdims=True)


def merge(parts):
    top = parts[0][1]
    for _, level in parts[1:]:
        top = jnp.maximum(top, level)
    weights = [jnp.exp2(level - top) for _, level in parts]
    total = weights[0]
    for w in weights[1:]:
        total = total + w
    mixed = parts[0][0] * weights[0]
    for (out, _), w in zip(parts[1:], weights[1:]):
        mixed = mixed + out * w
    return mixed / total, top + log2(total)


SCRATCH = {
    "kl": pltpu.VMEM((KEYS, HD), BF16),
    "kb": pltpu.VMEM((RING, 2 * HD, KEYS), BF16),
    "vb": pltpu.VMEM((RING, KEYS, HD), BF16),
    "qb": pltpu.VMEM((RING, GQ * SPAN, HD), BF16),
    "ts0": pltpu.VMEM((BLOCK, KEYS), F32),
    "ts1": pltpu.VMEM((BLOCK, KEYS), F32),
    "mx0": pltpu.VMEM((BLOCK, HD), F32),
    "mx1": pltpu.VMEM((BLOCK, HD), F32),
    "dq": pltpu.VMEM((ROWS, STEPS, GQ * HD), BF16),
    "nkv": pltpu.VMEM((2, ROWS, STEPS, HD), BF16),
    "acc": pltpu.VMEM((RING, GQ * SPAN, HD), F32),
    "top": pltpu.VMEM((RING, GQ * SPAN, HD), F32),
    "tot": pltpu.VMEM((RING, GQ * SPAN, HD), F32),
    "os": pltpu.VMEM((RING, GQ, SPAN, HD), BF16),
    "ls": pltpu.VMEM((RING, GQ, SPAN), F32),
    "orb": pltpu.VMEM((RING, GQ, SPAN, HD), BF16),
    "lrb": pltpu.VMEM((RING, GQ, SPAN), F32),
    "ck": pltpu.VMEM((ROWS, SLOTS, HD), BF16),
    "cv": pltpu.VMEM((ROWS, SLOTS, HD), BF16),
    "wb": pltpu.VMEM((GQ * HD, COLS), BF16),
    "qf": pltpu.VMEM((ROWS * QROWS, HD), F32),
    "kn": pltpu.VMEM((HD, HD), F32),
    "vn": pltpu.VMEM((HD, HD), F32),
    "of": pltpu.VMEM((ROWS * QROWS, HD), F32),
    "mf": pltpu.VMEM((ROWS * QROWS, HD), F32),
    "lf": pltpu.VMEM((ROWS * QROWS, HD), F32),
    "sb": pltpu.VMEM((RING, QROWS, HD), BF16),
    "sx": pltpu.VMEM((QROWS, HD), BF16),
    "xb": pltpu.VMEM((RING, QROWS, HD), BF16),
    "hos": pltpu.VMEM((QROWS, HD), BF16),
    "hls": pltpu.VMEM((8, HD), F32),
    "ho": pltpu.VMEM((RING, QROWS, HD), BF16),
    "hl": pltpu.VMEM((RING, 8, HD), F32),
    "sl": pltpu.VMEM((RING, 8, HD), F32),
    "ho2": pltpu.VMEM((RING, QROWS, HD), BF16),
    "hl2": pltpu.VMEM((RING, 16, HD), F32),
    "wt": pltpu.VMEM((2 * QROWS, HD), F32),
    "ot": pltpu.VMEM((2 * QROWS, HD), F32),
    "ab": pltpu.VMEM((RING, RING, GQ, ROWS * STEPS, HD), BF16),
    "am": pltpu.VMEM((RING * ROWS * STEPS, GQ * HD), BF16),
    "pr": pltpu.VMEM((RING * ROWS * STEPS, COLS), F32),
    "pm": pltpu.VMEM((RING, 128, COLS), F32),
    "so": pltpu.VMEM((RING, 128, COLS), BF16),
    "si": pltpu.VMEM((RING, 128, COLS), BF16),
    "xo": pltpu.VMEM((RING, 128, COLS), BF16),
    "xi": pltpu.VMEM((RING, 128, COLS), BF16),
    "own": pltpu.VMEM((128, COLS), F32),
    "clen": pltpu.SMEM((1, ROWS), jnp.int32),
    "loc": pltpu.SemaphoreType.DMA((18,)),
    "kvs": pltpu.SemaphoreType.DMA((6,)),
    "kr": pltpu.SemaphoreType.DMA((RING,)),
    "vr": pltpu.SemaphoreType.DMA((RING,)),
    "qs": pltpu.SemaphoreType.DMA((6,)),
    "qr": pltpu.SemaphoreType.DMA((RING,)),
    "bs": pltpu.SemaphoreType.DMA((RING,)),
    "br": pltpu.SemaphoreType.DMA((RING,)),
    "xs": pltpu.SemaphoreType.DMA((RING,)),
    "xr": pltpu.SemaphoreType.DMA((RING,)),
    "hs": pltpu.SemaphoreType.DMA((RING,)),
    "hr": pltpu.SemaphoreType.DMA((RING,)),
    "hls_s": pltpu.SemaphoreType.DMA((RING,)),
    "hlr": pltpu.SemaphoreType.DMA((RING,)),
    "sls": pltpu.SemaphoreType.DMA((RING,)),
    "slr": pltpu.SemaphoreType.DMA((RING,)),
    "h2s": pltpu.SemaphoreType.DMA((RING,)),
    "h2r": pltpu.SemaphoreType.DMA((RING,)),
    "hl2s": pltpu.SemaphoreType.DMA((RING,)),
    "hl2r": pltpu.SemaphoreType.DMA((RING,)),
    "as_": pltpu.SemaphoreType.DMA((RING,)),
    "ar": pltpu.SemaphoreType.DMA((RING,)),
    "ays": pltpu.SemaphoreType.DMA((6,)),
    "ayr": pltpu.SemaphoreType.DMA((RING, 2)),
    "ops": pltpu.SemaphoreType.DMA((RING,)),
    "opr": pltpu.SemaphoreType.DMA((RING,)),
    "lps": pltpu.SemaphoreType.DMA((RING,)),
    "lpr": pltpu.SemaphoreType.DMA((RING,)),
    "sis": pltpu.SemaphoreType.DMA((RING,)),
    "sir": pltpu.SemaphoreType.DMA((RING,)),
    "xis": pltpu.SemaphoreType.DMA((RING,)),
    "xir": pltpu.SemaphoreType.DMA((RING,)),
}


class Names:
    pass


def kernel(plen, prow, clen_in, q_in, skv, pkv, dq, nkv, cache, w_in, out_p, out_d, *scratch):
    s = Names()
    for name, ref in zip(SCRATCH, scratch):
        setattr(s, name, ref)

    me = lax.axis_index("ctx")
    y, z = lax.div(me, RING), lax.rem(me, RING)
    head = lax.axis_index("head")
    x, core = lax.div(head, 2), lax.rem(head, 2)
    other = 1 - lax.axis_index("grp")

    def turned(j):
        return lax.rem(y + lax.div(j * (j + 1), 2), RING)

    def near(p):
        high = lax.rem(lax.div(z, 2) + lax.div(p, 2), 2)
        return 2 * high + lax.rem(z + p, 2)

    up, down, far = lax.rem(y + 1, RING), lax.rem(y + 3, RING), lax.rem(y + 2, RING)

    def at_y(yy):
        return {"ctx": yy * RING + z}

    def at_z(zz):
        return {"ctx": y * RING + zz}

    def across(zz):
        return {"ctx": y * RING + zz, "grp": other}

    def at_x(xx):
        return {"head": xx * 2 + core}

    sibling = {"head": x * 2 + 1 - core}

    def send(src, dst, ssem, rsem, device):
        return pltpu.make_async_remote_copy(
            src_ref=src, dst_ref=dst, send_sem=ssem, recv_sem=rsem, device_id=device, device_id_type=MESH
        )

    def arrived(dst, rsem):
        send(dst, dst, s.loc.at[0], rsem, sibling).wait_recv()

    pairs = [
        (pkv.at[0], s.kl.at[pl.ds(0, PRE)]),
        (skv.at[0], s.kl.at[pl.ds(PRE, SPAN)]),
        (pkv.at[1], s.vb.at[y, pl.ds(0, PRE)]),
        (skv.at[1], s.vb.at[y, pl.ds(PRE, SPAN)]),
    ]
    pairs += [(q_in.at[:, pl.ds(h * HD, HD)], s.qb.at[z, pl.ds(h * SPAN, SPAN)]) for h in range(GQ)]
    pairs += [(dq, s.dq), (nkv, s.nkv), (clen_in, s.clen), (cache.at[0], s.ck), (cache.at[1], s.cv), (w_in, s.wb)]
    loads = [pltpu.make_async_copy(src, dst, s.loc.at[at]) for at, (src, dst) in enumerate(pairs)]
    for load in loads:
        load.start()

    barrier = pltpu.get_barrier_semaphore()
    greeted = [at_y(lax.rem(y + d, RING)) for d in (1, 2, 3)] + [at_z(lax.rem(z + d, RING)) for d in (1, 2, 3)]
    greeted += [across(zz) for zz in range(RING)] + [sibling] + [at_x(lax.rem(x + d, RING)) for d in (1, 2, 3)]
    for device in greeted:
        pl.semaphore_signal(barrier, inc=1, device_id=device, device_id_type=MESH)

    def clear(p, carry):
        s.acc[p] = jnp.zeros((GQ * SPAN, HD), F32)
        s.tot[p] = jnp.zeros((GQ * SPAN, HD), F32)
        s.top[p] = jnp.full((GQ * SPAN, HD), MASKED, F32)
        slot = iota((HD, KEYS), 1)
        unused = ((p * RING + z) * PRE + slot >= plen[0]) & (slot < PRE) & (iota((HD, KEYS), 0) == 0)
        s.kb[p, HD : 2 * HD, :] = jnp.where(unused, MASKED, 0.0).astype(BF16)
        return carry

    lax.fori_loop(0, RING, clear, 0)


    for load in loads[2:12]:
        load.wait()
    pl.semaphore_wait(barrier, len(greeted))

    def keys_of(yy):
        return s.kb.at[yy, pl.ds(0, HD)]

    kv_own = [
        send(s.vb.at[y], s.vb.at[y], s.kvs.at[0], s.vr.at[y], at_y(up)),
        send(s.vb.at[y], s.vb.at[y], s.kvs.at[1], s.vr.at[y], at_y(down)),
        send(keys_of(y), keys_of(y), s.kvs.at[2], s.kr.at[y], at_y(up)),
        send(keys_of(y), keys_of(y), s.kvs.at[3], s.kr.at[y], at_y(down)),
    ]
    kv_on = [
        send(keys_of(down), keys_of(down), s.kvs.at[4], s.kr.at[down], at_y(up)),
        send(s.vb.at[up], s.vb.at[up], s.kvs.at[5], s.vr.at[up], at_y(down)),
    ]

    def q_copy(source, step, sem):
        return send(s.qb.at[source], s.qb.at[source], s.qs.at[sem], s.qr.at[source], at_z(z + step))

    q_first = [(z < 3, z, 1, 0), (z > 0, z, -1, 1)]
    q_second = [((z > 0) & (z < 3), z - 1, 1, 2), ((z > 0) & (z < 3), z + 1, -1, 3)]
    q_third = [(z == 2, z - 2, 1, 4), (z == 1, z + 2, -1, 5)]

    def q_start(group):
        for when, source, step, sem in group:

            @pl.when(when)
            def _(source=source, step=step, sem=sem):
                q_copy(source, step, sem).start()

    def q_wait(distance):
        @pl.when(z >= distance)
        def _():
            arrived(s.qb.at[z - distance], s.qr.at[z - distance])

        @pl.when(z + distance < RING)
        def _():
            arrived(s.qb.at[z + distance], s.qr.at[z + distance])

    def b_copy(d):
        return send(s.sb.at[y], s.sb.at[y], s.bs.at[d], s.br.at[y], at_y(lax.rem(y + d, RING)))

    for copy in kv_own[:2]:
        copy.start()
    q_start(q_first)
    for load in loads[:2]:
        load.wait()
    s.kb[y, 0:HD, :] = s.kl[...].T
    for copy in kv_own[2:]:
        copy.start()

    for load in loads[12:15]:
        load.wait()
    for r in range(ROWS):
        row = s.dq[r].astype(F32)
        for h in range(GQ):
            s.qf[pl.ds(r * QROWS + h, STEPS, stride=GQ), :] = row[:, h * HD : (h + 1) * HD]
    s.kn[...] = jnp.zeros((HD, HD), F32)
    s.vn[...] = jnp.zeros((HD, HD), F32)
    for r in range(ROWS):
        s.kn[pl.ds(r * STEPS, STEPS), :] = s.nkv[0, r].astype(F32)
        s.vn[pl.ds(r * STEPS, STEPS), :] = s.nkv[1, r].astype(F32)

    def picked(ref):
        def add(r, total):
            mine = jnp.where(me * ROWS + r == prow[0], 1.0, 0.0)
            return total + mine * ref[pl.ds(pl.multiple_of(r * QROWS, QROWS), QROWS), :]

        return lax.fori_loop(0, ROWS, add, jnp.zeros((QROWS, HD), F32))

    s.sb[y] = picked(s.qf).astype(BF16)

    for d in (1, 2, 3):
        b_copy(d).start()

    lanes = (ROWS * QROWS, HD)
    at_row, at_key = iota(lanes, 0), iota(lanes, 1)
    same = lax.shift_right_logical(at_row, 5) == lax.shift_right_logical(at_key, 2)
    early = jnp.bitwise_and(at_key, 3) <= jnp.bitwise_and(lax.shift_right_logical(at_row, 3), 3)
    new = jnp.where(same & early, dot_nt(s.qf[...].astype(BF16), s.kn[...].astype(BF16)) * SCALE, MASKED)
    new_top = jnp.max(new, axis=1, keepdims=True)
    new_weights = jnp.exp2(new - new_top)
    s.mf[...] = jnp.broadcast_to(new_top, lanes)
    s.lf[...] = jnp.broadcast_to(jnp.sum(new_weights, axis=1, keepdims=True), lanes)
    s.of[...] = dot_nn(new_weights.astype(BF16), s.vn[...].astype(BF16))

    for load in loads[15:]:
        load.wait()

    def cached(r):
        rows = pl.ds(pl.multiple_of(r * QROWS, QROWS), QROWS)
        scores = dot_nt(s.qf[rows, :].astype(BF16), s.ck[r]) * SCALE
        scores = jnp.where(iota((QROWS, SLOTS), 1) < s.clen[0, r], scores, MASKED)
        before = s.mf[rows, :]
        after = jnp.maximum(before, jnp.max(scores, axis=1, keepdims=True))
        weights = jnp.exp2(scores - after[:, :1])
        keep = jnp.exp2(before - after)
        total = s.lf[rows, :] * keep + jnp.sum(weights, axis=1, keepdims=True)
        mixed = s.of[rows, :] * keep + dot_nn(weights.astype(BF16), s.cv[r])
        s.of[rows, :] = mixed / total
        s.lf[rows, :] = after + log2(total)

    def first_queries():
        q_wait(1)
        q_start(q_second)

    def some_rows(i, carry):
        @pl.when(i == 2)
        def _():
            first_queries()

        for u in range(4):
            cached(i * 4 + u)
        return carry

    lax.fori_loop(0, ROWS // 4, some_rows, 0)
    for h in range(GQ):
        s.ab[y, z, h] = s.of[pl.ds(h, ROWS * STEPS, stride=GQ), :].astype(BF16)

    def a_copy(d):
        return send(s.ab.at[y, z], s.ab.at[y, z], s.as_.at[d], s.ar.at[z], at_z(lax.rem(z + d, RING)))

    for d in (1, 2, 3):
        a_copy(d).start()
    s.sl[z] = jnp.broadcast_to(to_row(picked(s.lf)), (8, HD))

    def x_copy(d):
        zz = lax.rem(z + d, RING)
        return send(s.sx, s.xb.at[z], s.xs.at[d], s.xr.at[z], across(zz))

    def pass_query():
        for d in (1, 2, 3):
            yy = lax.rem(y + d, RING)
            arrived(s.sb.at[yy], s.br.at[yy])
        total = s.sb[0].astype(F32)
        for yy in (1, 2, 3):
            total = total + s.sb[yy].astype(F32)
        s.sx[...] = total.astype(BF16)
        for d in range(RING):
            x_copy(d).start()

    def h_copies(d):
        zz = lax.rem(z + d, RING)
        copies = [
            send(s.hos, s.ho.at[z], s.hs.at[d], s.hr.at[z], across(zz)),
            send(s.hls, s.hl.at[z], s.hls_s.at[d], s.hlr.at[z], across(zz)),
        ]
        if d:
            copies.append(send(s.sl.at[z], s.sl.at[z], s.sls.at[d], s.slr.at[z], at_z(zz)))
        return copies

    def answer():
        for zz in range(RING):
            arrived(s.xb.at[zz], s.xr.at[zz])
        query = s.xb[0].astype(F32)
        for zz in (1, 2, 3):
            query = query + s.xb[zz].astype(F32)
        span = pl.ds(PRE, SPAN)
        scores = dot_nn(query.astype(BF16), s.kb[y, 0:HD, span]) * SCALE
        top = jnp.max(scores, axis=1, keepdims=True)
        weights = jnp.exp2(scores - top)
        total = jnp.sum(weights, axis=1, keepdims=True)
        s.hos[...] = (dot_nn(weights.astype(BF16), s.vb[y, span, :]) / total).astype(BF16)
        level = jnp.broadcast_to(top + log2(total), (QROWS, HD))
        s.hls[...] = jnp.broadcast_to(to_row(level), (8, HD))
        for d in range(RING):
            for copy in h_copies(d):
                copy.start()

    def h2_copies(d):
        yy = lax.rem(y + d, RING)
        return [
            send(s.ho2.at[y], s.ho2.at[y], s.h2s.at[d], s.h2r.at[y], at_y(yy)),
            send(s.hl2.at[y], s.hl2.at[y], s.hl2s.at[d], s.hl2r.at[y], at_y(yy)),
        ]

    def combine_z():
        for zz in range(RING):
            arrived(s.ho.at[zz], s.hr.at[zz])
            arrived(s.hl.at[zz], s.hlr.at[zz])
        for d in (1, 2, 3):
            zz = lax.rem(z + d, RING)
            arrived(s.sl.at[zz], s.slr.at[zz])
        out, level = merge([(s.ho[zz].astype(F32), to_column(s.hl[zz, 0:1, :], QROWS)) for zz in range(RING)])
        s.ho2[y] = out.astype(BF16)
        s.hl2[y, 0:8, :] = jnp.broadcast_to(to_row(jnp.broadcast_to(level, (QROWS, HD))), (8, HD))
        s.hl2[y, 8:16, :] = s.sl[0] + s.sl[1] + s.sl[2] + s.sl[3]
        for d in (1, 2, 3):
            for copy in h2_copies(d):
                copy.start()

    def combine_y():
        for d in (1, 2, 3):
            yy = lax.rem(y + d, RING)
            arrived(s.ho2.at[yy], s.h2r.at[yy])
            arrived(s.hl2.at[yy], s.hl2r.at[yy])
        out, level = merge([(s.ho2[yy].astype(F32), to_column(s.hl2[yy, 0:1, :], QROWS)) for yy in range(RING)])
        rows = s.hl2[0, 8:9, :] + s.hl2[1, 8:9, :] + s.hl2[2, 8:9, :] + s.hl2[3, 8:9, :]
        before = to_column(rows, QROWS)
        top = jnp.maximum(before, level)
        w_own, w_span = jnp.exp2(before - top), jnp.exp2(level - top)
        total = w_own + w_span
        keep = jnp.broadcast_to(w_own / total, (QROWS, HD))
        added = out * (w_span / total)
        for at in range(2):
            s.wt[pl.ds(at * QROWS, QROWS), :] = keep
            s.ot[pl.ds(at * QROWS, QROWS), :] = added

    def half(yy, i):
        return s.ab.at[yy, pl.ds(2 * i, 2)]

    def ay_copy(yy, i, sem, to):
        return send(half(yy, i), half(yy, i), s.ays.at[sem], s.ayr.at[yy, i], at_y(to))

    ay_own = [ay_copy(y, 0, 0, up), ay_copy(y, 1, 1, down), ay_copy(y, 1, 2, up), ay_copy(y, 0, 3, down)]
    ay_on = [ay_copy(down, 0, 4, up), ay_copy(up, 1, 5, down)]

    def spread_rows():
        for d in (1, 2, 3):
            zz = lax.rem(z + d, RING)
            arrived(s.ab.at[y, zz], s.ar.at[zz])
        for copy in ay_own:
            copy.start()

    def pass_rows():
        arrived(half(down, 0), s.ayr.at[down, 0])
        ay_on[0].start()
        arrived(half(up, 1), s.ayr.at[up, 1])
        ay_on[1].start()

    def rest_of_rows():
        arrived(half(down, 1), s.ayr.at[down, 1])
        arrived(half(up, 0), s.ayr.at[up, 0])

    def far_rows():
        for i in range(2):
            arrived(half(far, i), s.ayr.at[far, i])

    def si_copy(j):
        return send(s.so.at[j], s.si.at[j], s.sis.at[j], s.sir.at[j], sibling)

    def project(j):
        yc = turned(j)
        count = RING * ROWS * STEPS
        row = yc * (RING * ROWS) + lax.shift_right_logical(iota((count, HD), 0), 2)
        hit = row == prow[0]
        for h in range(GQ):
            block = jnp.concatenate([s.ab[yc, zz, h] for zz in range(RING)], axis=0).astype(F32)
            keep = s.wt[pl.ds(h, 2 * STEPS, stride=GQ), :]
            added = s.ot[pl.ds(h, 2 * STEPS, stride=GQ), :]
            keep = jnp.concatenate([keep] * (count // (2 * STEPS)), axis=0)
            added = jnp.concatenate([added] * (count // (2 * STEPS)), axis=0)
            block = jnp.where(hit, block * keep + added, block)
            s.am[:, h * HD : (h + 1) * HD] = block.astype(BF16)
        s.pr[...] = dot_nn(s.am[...], s.wb[...])
        s.pm[j] = s.pr[pl.ds(pl.multiple_of(core * 128, 128), 128), :]
        s.so[j] = s.pr[pl.ds(pl.multiple_of((1 - core) * 128, 128), 128), :].astype(BF16)
        si_copy(j).start()

    def xi_copy(j):
        return send(s.xo.at[j], s.xi.at[x], s.xis.at[j], s.xir.at[x], at_x(turned(j)))

    def join(j):
        arrived(s.si.at[j], s.sir.at[j])
        total = s.pm[j] + s.si[j].astype(F32)

        @pl.when(turned(j) == x)
        def _():
            s.own[...] = total

        @pl.when(turned(j) != x)
        def _():
            s.xo[j] = total.astype(BF16)
            xi_copy(j).start()

    count = BLOCK // SPAN
    first_lane = jnp.where(iota((BLOCK, HD), 1) == 0, 1.0, 0.0).astype(BF16)
    ones = jnp.ones((KEYS, HD), BF16)

    def scores_of(at, b, held, peak):
        p, yc = lookup(PIECES, at), turned(lookup(CHUNKS, at))
        zq = near(p)
        late = (y * RING + zq) * SPAN - (yc * RING + z) * SPAN
        shape = (SPAN, SPAN)
        ahead = jnp.where(iota(shape, 1) - iota(shape, 0) <= late, 0.0, MASKED)
        ahead = jnp.concatenate([ahead] * count, axis=0)
        queries = jnp.concatenate([s.qb[zq, b * BLOCK : (b + 1) * BLOCK, :], first_lane], axis=1)
        scores = dot_nn(queries, s.kb[yc])
        highest = None
        for k in range(KEYS // HD):
            cols = slice(k * HD, (k + 1) * HD)
            part = scores[:, cols] * SCALE
            if k == PRE // HD:
                part = part + ahead
            held[:, cols] = part
            highest = part if highest is None else jnp.maximum(highest, part)
        peak[...] = jnp.broadcast_to(jnp.max(highest, axis=1, keepdims=True), (BLOCK, HD))

    def weigh(at, b, held, peak):
        p, yc = lookup(PIECES, at), turned(lookup(CHUNKS, at))
        rows = slice(b * BLOCK, (b + 1) * BLOCK)
        before = s.top[p, rows, :]
        after = jnp.maximum(before, peak[...])
        keep = jnp.exp2(before - after)
        packed = []
        for k in range(KEYS // HD):
            packed.append(jnp.exp2(held[:, k * HD : (k + 1) * HD] - after).astype(BF16))
        mixed = dot_nn(jnp.concatenate(packed, axis=1), jnp.concatenate([s.vb[yc], ones], axis=1))
        s.top[p, rows, :] = after
        s.tot[p, rows, :] = s.tot[p, rows, :] * keep + mixed[:, HD:]
        s.acc[p, rows, :] = s.acc[p, rows, :] * keep + mixed[:, :HD]

    def o_copies(p):
        return [
            send(s.os.at[p], s.orb.at[p], s.ops.at[p], s.opr.at[p], at_z(near(p))),
            send(s.ls.at[p], s.lrb.at[p], s.lps.at[p], s.lpr.at[p], at_z(near(p))),
        ]

    def ship(p):
        def one(h, carry):
            rows = pl.ds(pl.multiple_of(h * SPAN, SPAN), SPAN)
            total = s.tot[p, rows, :]
            s.os[p, h] = (s.acc[p, rows, :] / total).astype(BF16)
            s.ls[p, pl.ds(h, 1), :] = to_row(s.top[p, rows, :] + log2(total))
            return carry

        lax.fori_loop(0, GQ, one, 0)
        for copy in o_copies(p):
            copy.start()

    def settle():
        def one(h, carry):
            rows = pl.ds(pl.multiple_of(h * SPAN, SPAN), SPAN)
            levels = [to_column(s.lrb[p, pl.ds(h, 1), :], SPAN) for p in (1, 2, 3)]
            top = s.top[0, rows, :]
            for level in levels:
                top = jnp.maximum(top, level)
            weight = jnp.exp2(s.top[0, rows, :] - top)
            total = s.tot[0, rows, :] * weight
            mixed = s.acc[0, rows, :] * weight
            for p, level in zip((1, 2, 3), levels):
                weight = jnp.exp2(level - top)
                total = total + weight
                mixed = mixed + s.orb[p, h].astype(F32) * weight
            out_p[:, pl.ds(pl.multiple_of(h * HD, HD), HD)] = (mixed / total).astype(BF16)
            return carry

        lax.fori_loop(0, GQ, one, 0)

    def keys_near():
        arrived(keys_of(down), s.kr.at[down])
        kv_on[0].start()
        arrived(s.vb.at[up], s.vr.at[up])
        kv_on[1].start()
        arrived(s.vb.at[down], s.vr.at[down])
        arrived(keys_of(up), s.kr.at[up])

    def keys_far():
        arrived(keys_of(far), s.kr.at[far])
        arrived(s.vb.at[far], s.vr.at[far])

    def second_queries():
        q_wait(2)
        q_start(q_third)

    actions = {
        0: [pass_query],
        2: [keys_near],
        3: [answer],
        4: [second_queries],
        6: [combine_z],
        7: [keys_far, spread_rows],
        8: [lambda: q_wait(3)],
        9: [combine_y],
        11: [pass_rows],
        14: [rest_of_rows],
        16: [far_rows],
    }

    def prepare(i):
        for at, todo in actions.items():

            @pl.when(i == at)
            def _(todo=todo):
                for action in todo:
                    action()

        @pl.when(i >= 14)
        def _():
            join(i - 14)

        @pl.when((i == 12) | (i >= 14))
        def _():
            project(jnp.maximum(i - 13, 0))

    def step(i, carry):
        scores_of(i, 1, s.ts1, s.mx1)
        weigh(i, 0, s.ts0, s.mx0)
        prepare(i + 1)
        scores_of(jnp.minimum(i + 1, 15), 0, s.ts0, s.mx0)
        weigh(i, 1, s.ts1, s.mx1)
        p, k = lookup(PIECES, i), lookup(CHUNKS, i)

        @pl.when((k == 3) & (p > 0))
        def _():
            ship(p)

        return carry

    for action in actions.pop(0):
        action()
    scores_of(0, 0, s.ts0, s.mx0)
    lax.fori_loop(0, 16, step, 0)
    join(RING - 1)

    for p in (1, 2, 3):
        arrived(s.orb.at[p], s.opr.at[p])
        arrived(s.lrb.at[p], s.lpr.at[p])
    settle()

    total = s.own[...]
    for d in (1, 2, 3):
        xx = lax.rem(x + d, RING)
        arrived(s.xi.at[xx], s.xir.at[xx])
        total = total + s.xi[xx].astype(F32)
    for r in range(32):
        out_d[r] = total[r * STEPS : (r + 1) * STEPS, :].astype(BF16)

    for copy in kv_own + kv_on + ay_own + ay_on:
        copy.wait_send()
    for when, source, step_z, sem in q_first + q_second + q_third:

        @pl.when(when)
        def _(source=source, step_z=step_z, sem=sem):
            q_copy(source, step_z, sem).wait_send()

    for d in range(RING):
        x_copy(d).wait_send()
        for copy in h_copies(d):
            copy.wait_send()
        if d:
            b_copy(d).wait_send()
            a_copy(d).wait_send()
            for copy in h2_copies(d):
                copy.wait_send()
            for copy in o_copies(d):
                copy.wait_send()
    for j in range(RING):
        si_copy(j).wait_send()

        @pl.when(turned(j) != x)
        def _(j=j):
            xi_copy(j).wait_send()


def shards(span_q, span_kv, prefix_kv, prefix_len, dec_q, dec_new_kv, dec_cache, cache_len, prompt_row, out_weight):
    vmem = pl.BlockSpec(memory_space=pltpu.VMEM)
    smem = pl.BlockSpec(memory_space=pltpu.SMEM)
    hbm = pl.BlockSpec(memory_space=pltpu.HBM)
    prefill, decode = pl.pallas_call(
        kernel,
        out_shape=(
            jax.ShapeDtypeStruct((SPAN, GQ * HD), BF16),
            jax.ShapeDtypeStruct((32, STEPS, COLS), BF16),
        ),
        in_specs=[smem] * 2 + [hbm] * 8,
        out_specs=(vmem, vmem),
        scratch_shapes=list(SCRATCH.values()),
        compiler_params=pltpu.CompilerParams(
            collective_id=0, has_side_effects=True, vmem_limit_bytes=VMEM_BYTES
        ),
        cost_estimate=pl.CostEstimate(flops=11_000_000_000, bytes_accessed=8_000_000, transcendentals=17_000_000),
    )(
        prefix_len,
        prompt_row,
        *[
            pltpu.with_memory_space_constraint(operand, pltpu.HBM)
            for operand in (
                cache_len,
                span_q[0],
                span_kv[0],
                prefix_kv[0],
                dec_q[0],
                dec_new_kv[0],
                dec_cache[0],
                out_weight,
            )
        ],
    )
    return prefill[None], decode[None]


def solution(mesh):
    placed = (
        P("grp", "ctx", "head"),
        P("grp", None, "ctx", "head"),
        P("grp", None, "ctx", "head"),
        P("grp"),
        P("grp", "ctx", None, "head"),
        P("grp", None, "ctx", None, "head"),
        P("grp", None, "ctx", None, "head"),
        P("grp", "ctx"),
        P("grp"),
        P("head", "ctx"),
    )
    return jax.shard_map(
        shards,
        mesh=mesh,
        in_specs=placed,
        out_specs=(P("grp", "ctx", "head"), P("grp", "head", None, "ctx")),
        check_vma=False,
    )
```

time: 503 us -> 77.8 us (0.15)
  waiting for transfers between devices: 374 us -> 0 us
  Pallas kernels: 0 us -> 74.3 us
  matrix products: 65.4 us -> 0 us
  other arithmetic: 31.8 us -> 0 us
  between operations: 15.3 us -> 1.93 us
  starting transfers between devices: 7.62 us -> 0 us
    all_gather x3 -> x0, waiting for transfers between devices: 339 us -> none  [the longest x1 185 us: shards(): shard_piece = lax.all_gather(local_kv, 'ctx', axis=1, tiled=True)]
    pallas_call x0 -> x1, Pallas kernels: none -> 74.3 us  [shards(): pl.pallas_call(kernel, out_shape=(jax.ShapeDtypeStruct((SPAN, GQ * HD), B...]
    dot_general x9 -> x0, matrix products: 65.4 us -> none  [the longest x4 29.9 us: absorb(): jnp.einsum(einsum_form, weights.astype(jnp.bfloat16), values, preferred_e...]
    reduce_scatter x1 -> x0, waiting for transfers between devices: 31.5 us -> none  [shards(): lax.psum_scatter(partial_terms.astype(jnp.bfloat16), 'head', scatter_dime...]
    reduce_sum x4 -> x0, other arithmetic: 22.2 us -> none  [absorb(): row_total = row_total * rescale + jnp.sum(weights, axis=-1)]
    select_n x1 -> x0, other arithmetic: 7.82 us -> none  [shards(): usable = jnp.where((within < prefix_rows)[None], prefix_ok[None], span_ok)]
    ppermute x1 -> x0, starting transfers between devices: 7.28 us -> none  [swapped(): return lax.ppermute(block, axis, route)]
  transfers between devices with their start and end apart: 5 -> 0, of which waited for: 5 -> 0; matrix products, arithmetic and copies ran while one was open for 4% -> 0% of each run, Pallas kernels for 0% -> 0%
where the time goes in v1:
time: 77.8 us; the launch traced here: 77.6 us
  Pallas kernels  74.3 us (96%)
  between operations  1.93 us (2%)
  local copies, waits for them, and re-layouts  1.36 us (2%)
    pallas_call x1, Pallas kernels, shards(): pl.pallas_call(kernel, out_shape=(jax.ShapeDtypeStruct((SPAN, GQ * HD), B...  74.3 us

profile of v1, /device:TPU:16, one launch (start us, length us, event | category | flops | bytes accessed | tf_op | source)
XLA Modules:
  0.0 77.6 jit_solution(11119654439922826301)
XLA Ops:
  1.9 74.3 %shard_map.113 = (bf16[128,1024]{1,0:T(8,128)(2,1)S(1)}, bf16[32,4,512]{2,1,0:T(4,128)(2,1)S(1)}) custom-call(s32[1]{0:T(128)S(6)} %copy.14.plen, s32[1]{0:T(128)S(6)} %copy.15.prow, s32[1,16]{1,0:T(1,128)} %clen_in.1, bf16[128,1024]{1,0:T(8,128)(2,1)} %bitcast.12, bf16[2,128,128]{2,1,0:T(8,128)(2,1)} %bitcast.14, bf16[2,896,128]{2,1,0:T(8,128)(2,1)} %bitcast.11, ...), custom_call_target="tpu_custom_call" | custom-call | flops 11000000512 | bytes 8000000 | tf_op jit(solution)/shard_map/pallas_call | solution.py:703
  76.2 0.7 copy.16
  76.9 0.7 copy.17

commit v2 on v1

--- a/solution.py
+++ b/solution.py
@@ -86,8 +86,10 @@
     "qb": pltpu.VMEM((RING, GQ * SPAN, HD), BF16),
     "ts0": pltpu.VMEM((BLOCK, KEYS), F32),
     "ts1": pltpu.VMEM((BLOCK, KEYS), F32),
-    "mx0": pltpu.VMEM((BLOCK, HD), F32),
-    "mx1": pltpu.VMEM((BLOCK, HD), F32),
+    "kp0": pltpu.VMEM((BLOCK, HD), F32),
+    "kp1": pltpu.VMEM((BLOCK, HD), F32),
+    "pk0": pltpu.VMEM((BLOCK, KEYS), BF16),
+    "pk1": pltpu.VMEM((BLOCK, KEYS), BF16),
     "dq": pltpu.VMEM((ROWS, STEPS, GQ * HD), BF16),
     "nkv": pltpu.VMEM((2, ROWS, STEPS, HD), BF16),
     "acc": pltpu.VMEM((RING, GQ * SPAN, HD), F32),
@@ -520,38 +522,64 @@
     first_lane = jnp.where(iota((BLOCK, HD), 1) == 0, 1.0, 0.0).astype(BF16)
     ones = jnp.ones((KEYS, HD), BF16)
 
-    def scores_of(at, b, held, peak):
+    def scores_of(at, b, held):
         p, yc = lookup(PIECES, at), turned(lookup(CHUNKS, at))
         zq = near(p)
-        late = (y * RING + zq) * SPAN - (yc * RING + z) * SPAN
-        shape = (SPAN, SPAN)
-        ahead = jnp.where(iota(shape, 1) - iota(shape, 0) <= late, 0.0, MASKED)
-        ahead = jnp.concatenate([ahead] * count, axis=0)
         queries = jnp.concatenate([s.qb[zq, b * BLOCK : (b + 1) * BLOCK, :], first_lane], axis=1)
-        scores = dot_nn(queries, s.kb[yc])
-        highest = None
-        for k in range(KEYS // HD):
-            cols = slice(k * HD, (k + 1) * HD)
-            part = scores[:, cols] * SCALE
-            if k == PRE // HD:
-                part = part + ahead
-            held[:, cols] = part
-            highest = part if highest is None else jnp.maximum(highest, part)
-        peak[...] = jnp.broadcast_to(jnp.max(highest, axis=1, keepdims=True), (BLOCK, HD))
-
-    def weigh(at, b, held, peak):
+
+        def quarter(j):
+            scores = dot_nn(queries, s.kb[yc, :, 2 * j * HD : 2 * (j + 1) * HD])
+            for k in (2 * j, 2 * j + 1):
+                part = scores[:, (k - 2 * j) * HD : (k - 2 * j + 1) * HD] * SCALE
+                if k == PRE // HD:
+                    late = (y * RING + zq) * SPAN - (yc * RING + z) * SPAN
+                    shape = (SPAN, SPAN)
+                    ahead = jnp.where(iota(shape, 1) - iota(shape, 0) <= late, 0.0, MASKED)
+                    part = part + jnp.concatenate([ahead] * count, axis=0)
+                held[:, k * HD : (k + 1) * HD] = part
+
+        return quarter
+
+    def weigh(at, b, held, keeps, packed):
+        p = lookup(PIECES, at)
+
+        def quarter(j):
+            for i in range(j * SPAN, (j + 1) * SPAN, 32):
+                mine = slice(i, i + 32)
+                rows = slice(b * BLOCK + i, b * BLOCK + i + 32)
+                tiles = [held[mine, k * HD : (k + 1) * HD] for k in range(KEYS // HD)]
+                highest = tiles[0]
+                for part in tiles[1:]:
+                    highest = jnp.maximum(highest, part)
+                before = s.top[p, rows, :]
+                after = jnp.maximum(before, jnp.max(highest, axis=1, keepdims=True))
+                s.top[p, rows, :] = after
+                keeps[mine, :] = jnp.exp2(before - after)
+                for k, part in enumerate(tiles):
+                    packed[mine, k * HD : (k + 1) * HD] = jnp.exp2(part - after).astype(BF16)
+
+        return quarter
+
+    def mix(at, b, keeps, packed):
         p, yc = lookup(PIECES, at), turned(lookup(CHUNKS, at))
-        rows = slice(b * BLOCK, (b + 1) * BLOCK)
-        before = s.top[p, rows, :]
-        after = jnp.maximum(before, peak[...])
-        keep = jnp.exp2(before - after)
-        packed = []
-        for k in range(KEYS // HD):
-            packed.append(jnp.exp2(held[:, k * HD : (k + 1) * HD] - after).astype(BF16))
-        mixed = dot_nn(jnp.concatenate(packed, axis=1), jnp.concatenate([s.vb[yc], ones], axis=1))
-        s.top[p, rows, :] = after
-        s.tot[p, rows, :] = s.tot[p, rows, :] * keep + mixed[:, HD:]
-        s.acc[p, rows, :] = s.acc[p, rows, :] * keep + mixed[:, :HD]
+
+        def half_block(j):
+            size = BLOCK // 2
+            mine = slice(j * size, (j + 1) * size)
+            rows = slice(b * BLOCK + j * size, b * BLOCK + (j + 1) * size)
+            mixed = dot_nn(packed[mine, :], jnp.concatenate([s.vb[yc], ones], axis=1))
+            keep = keeps[mine, :]
+            s.tot[p, rows, :] = s.tot[p, rows, :] * keep + mixed[:, HD:]
+            s.acc[p, rows, :] = s.acc[p, rows, :] * keep + mixed[:, :HD]
+
+        return half_block
+
+    def together(scores, weights, products):
+        for j in range(4):
+            scores(j)
+            weights(j)
+            if j % 2 == 0:
+                products(j // 2)
 
     def o_copies(p):
         return [
@@ -559,20 +587,27 @@
             send(s.ls.at[p], s.lrb.at[p], s.lps.at[p], s.lpr.at[p], at_z(near(p))),
         ]
 
+    def each_head(one):
+        def some(i, carry):
+            for u in range(4):
+                one(i * 4 + u)
+            return carry
+
+        lax.fori_loop(0, GQ // 4, some, 0)
+
     def ship(p):
-        def one(h, carry):
+        def one(h):
             rows = pl.ds(pl.multiple_of(h * SPAN, SPAN), SPAN)
             total = s.tot[p, rows, :]
             s.os[p, h] = (s.acc[p, rows, :] / total).astype(BF16)
             s.ls[p, pl.ds(h, 1), :] = to_row(s.top[p, rows, :] + log2(total))
-            return carry
-
-        lax.fori_loop(0, GQ, one, 0)
+
+        each_head(one)
         for copy in o_copies(p):
             copy.start()
 
     def settle():
-        def one(h, carry):
+        def one(h):
             rows = pl.ds(pl.multiple_of(h * SPAN, SPAN), SPAN)
             levels = [to_column(s.lrb[p, pl.ds(h, 1), :], SPAN) for p in (1, 2, 3)]
             top = s.top[0, rows, :]
@@ -586,9 +621,8 @@
                 total = total + weight
                 mixed = mixed + s.orb[p, h].astype(F32) * weight
             out_p[:, pl.ds(pl.multiple_of(h * HD, HD), HD)] = (mixed / total).astype(BF16)
-            return carry
-
-        lax.fori_loop(0, GQ, one, 0)
+
+        each_head(one)
 
     def keys_near():
         arrived(keys_of(down), s.kr.at[down])
@@ -636,24 +670,33 @@
         def _():
             project(jnp.maximum(i - 13, 0))
 
+    even = (s.ts0, s.kp0, s.pk0)
+    odd = (s.ts1, s.kp1, s.pk1)
+
     def step(i, carry):
-        scores_of(i, 1, s.ts1, s.mx1)
-        weigh(i, 0, s.ts0, s.mx0)
-        prepare(i + 1)
-        scores_of(jnp.minimum(i + 1, 15), 0, s.ts0, s.mx0)
-        weigh(i, 1, s.ts1, s.mx1)
-        p, k = lookup(PIECES, i), lookup(CHUNKS, i)
+        last = jnp.maximum(i - 1, 0)
+        together(scores_of(i, 1, odd[0]), weigh(i, 0, *even), mix(last, 1, *odd[1:]))
+        p, k = lookup(PIECES, last), lookup(CHUNKS, last)
 
         @pl.when((k == 3) & (p > 0))
         def _():
             ship(p)
 
+        prepare(i + 1)
+        together(scores_of(jnp.minimum(i + 1, 15), 0, even[0]), weigh(i, 1, *odd), mix(i, 0, *even[1:]))
         return carry
 
+    s.kp1[...] = jnp.ones((BLOCK, HD), F32)
+    s.pk1[...] = jnp.zeros((BLOCK, KEYS), BF16)
     for action in actions.pop(0):
         action()
-    scores_of(0, 0, s.ts0, s.mx0)
+    first = scores_of(0, 0, s.ts0)
+    for j in range(4):
+        first(j)
     lax.fori_loop(0, 16, step, 0)
+    rest = mix(15, 1, *odd[1:])
+    for j in range(2):
+        rest(j)
     join(RING - 1)
 
     for p in (1, 2, 3):

time: 77.8 us -> 79.5 us (1.022)
  Pallas kernels: 74.3 us -> 76.1 us
    pallas_call x1, Pallas kernels: 74.3 us -> 76.1 us  [shards(): pl.pallas_call(kernel, out_shape=(jax.ShapeDtypeStruct((SPAN, GQ * HD), B...]
where the time goes in v2:
time: 79.5 us; the launch traced here: 79.4 us
  Pallas kernels  76.1 us (96%)
  between operations  1.93 us (2%)
  local copies, waits for them, and re-layouts  1.36 us (2%)
    pallas_call x1, Pallas kernels, shards(): pl.pallas_call(kernel, out_shape=(jax.ShapeDtypeStruct((SPAN, GQ * HD), B...  76.1 us

profile of v2, /device:TPU:16, one launch (start us, length us, event | category | flops | bytes accessed | tf_op | source)
XLA Modules:
  0.0 79.4 jit_solution(6389559279359062217)
XLA Ops:
  1.9 76.1 %shard_map.113 = (bf16[128,1024]{1,0:T(8,128)(2,1)S(1)}, bf16[32,4,512]{2,1,0:T(4,128)(2,1)S(1)}) custom-call(s32[1]{0:T(128)S(6)} %copy.14.plen, s32[1]{0:T(128)S(6)} %copy.15.prow, s32[1,16]{1,0:T(1,128)} %clen_in.1, bf16[128,1024]{1,0:T(8,128)(2,1)} %bitcast.12, bf16[2,128,128]{2,1,0:T(8,128)(2,1)} %bitcast.14, bf16[2,896,128]{2,1,0:T(8,128)(2,1)} %bitcast.11, ...), custom_call_target="tpu_custom_call" | custom-call | flops 11000000512 | bytes 8000000 | tf_op jit(solution)/shard_map/pallas_call | solution.py:746
  78.0 0.7 copy.16
  78.7 0.7 copy.17

commit v3 on v1

--- a/solution.py
+++ b/solution.py
@@ -150,8 +150,8 @@
     "hl2r": pltpu.SemaphoreType.DMA((RING,)),
     "as_": pltpu.SemaphoreType.DMA((RING,)),
     "ar": pltpu.SemaphoreType.DMA((RING,)),
-    "ays": pltpu.SemaphoreType.DMA((6,)),
-    "ayr": pltpu.SemaphoreType.DMA((RING, 2)),
+    "ays": pltpu.SemaphoreType.DMA((3 * RING,)),
+    "ayr": pltpu.SemaphoreType.DMA((RING, RING)),
     "ops": pltpu.SemaphoreType.DMA((RING,)),
     "opr": pltpu.SemaphoreType.DMA((RING,)),
     "lps": pltpu.SemaphoreType.DMA((RING,)),
@@ -360,11 +360,43 @@
     for h in range(GQ):
         s.ab[y, z, h] = s.of[pl.ds(h, ROWS * STEPS, stride=GQ), :].astype(BF16)
 
-    def a_copy(d):
-        return send(s.ab.at[y, z], s.ab.at[y, z], s.as_.at[d], s.ar.at[z], at_z(lax.rem(z + d, RING)))
-
-    for d in (1, 2, 3):
-        a_copy(d).start()
+    def a_copy(p):
+        return send(s.ab.at[y, z], s.ab.at[y, z], s.as_.at[p], s.ar.at[z], at_z(near(p)))
+
+    def ay_copy(yy, p, sem, to):
+        block = s.ab.at[yy, near(p)]
+        return send(block, block, s.ays.at[sem], s.ayr.at[yy, near(p)], at_y(to))
+
+    def ay_own(p):
+        return [ay_copy(y, p, 3 * p, up), ay_copy(y, p, 3 * p + 1, down)]
+
+    def ay_on(p):
+        return ay_copy(down, p, 3 * p + 2, up) if p < 2 else ay_copy(up, p, 3 * p + 2, down)
+
+    def rows_in(yy, p):
+        arrived(s.ab.at[yy, near(p)], s.ayr.at[yy, near(p)])
+
+    def spread_rows(p):
+        if p:
+            arrived(s.ab.at[y, near(p)], s.ar.at[near(p)])
+        for copy in ay_own(p):
+            copy.start()
+
+    def pass_rows(p):
+        rows_in(down if p < 2 else up, p)
+        ay_on(p).start()
+
+    def rest_of_rows():
+        for p in range(RING):
+            rows_in(up if p < 2 else down, p)
+
+    def far_rows():
+        for p in range(RING):
+            rows_in(far, p)
+
+    for p in (1, 2, 3):
+        a_copy(p).start()
+    spread_rows(0)
     s.sl[z] = jnp.broadcast_to(to_row(picked(s.lf)), (8, HD))
 
     def x_copy(d):
@@ -448,36 +480,6 @@
         for at in range(2):
             s.wt[pl.ds(at * QROWS, QROWS), :] = keep
             s.ot[pl.ds(at * QROWS, QROWS), :] = added
-
-    def half(yy, i):
-        return s.ab.at[yy, pl.ds(2 * i, 2)]
-
-    def ay_copy(yy, i, sem, to):
-        return send(half(yy, i), half(yy, i), s.ays.at[sem], s.ayr.at[yy, i], at_y(to))
-
-    ay_own = [ay_copy(y, 0, 0, up), ay_copy(y, 1, 1, down), ay_copy(y, 1, 2, up), ay_copy(y, 0, 3, down)]
-    ay_on = [ay_copy(down, 0, 4, up), ay_copy(up, 1, 5, down)]
-
-    def spread_rows():
-        for d in (1, 2, 3):
-            zz = lax.rem(z + d, RING)
-            arrived(s.ab.at[y, zz], s.ar.at[zz])
-        for copy in ay_own:
-            copy.start()
-
-    def pass_rows():
-        arrived(half(down, 0), s.ayr.at[down, 0])
-        ay_on[0].start()
-        arrived(half(up, 1), s.ayr.at[up, 1])
-        ay_on[1].start()
-
-    def rest_of_rows():
-        arrived(half(down, 1), s.ayr.at[down, 1])
-        arrived(half(up, 0), s.ayr.at[up, 0])
-
-    def far_rows():
-        for i in range(2):
-            arrived(half(far, i), s.ayr.at[far, i])
 
     def si_copy(j):
         return send(s.so.at[j], s.si.at[j], s.sis.at[j], s.sir.at[j], sibling)
@@ -559,20 +561,27 @@
             send(s.ls.at[p], s.lrb.at[p], s.lps.at[p], s.lpr.at[p], at_z(near(p))),
         ]
 
+    def each_head(one):
+        def some(i, carry):
+            for u in range(4):
+                one(i * 4 + u)
+            return carry
+
+        lax.fori_loop(0, GQ // 4, some, 0)
+
     def ship(p):
-        def one(h, carry):
+        def one(h):
             rows = pl.ds(pl.multiple_of(h * SPAN, SPAN), SPAN)
             total = s.tot[p, rows, :]
             s.os[p, h] = (s.acc[p, rows, :] / total).astype(BF16)
             s.ls[p, pl.ds(h, 1), :] = to_row(s.top[p, rows, :] + log2(total))
-            return carry
-
-        lax.fori_loop(0, GQ, one, 0)
+
+        each_head(one)
         for copy in o_copies(p):
             copy.start()
 
     def settle():
-        def one(h, carry):
+        def one(h):
             rows = pl.ds(pl.multiple_of(h * SPAN, SPAN), SPAN)
             levels = [to_column(s.lrb[p, pl.ds(h, 1), :], SPAN) for p in (1, 2, 3)]
             top = s.top[0, rows, :]
@@ -586,9 +595,8 @@
                 total = total + weight
                 mixed = mixed + s.orb[p, h].astype(F32) * weight
             out_p[:, pl.ds(pl.multiple_of(h * HD, HD), HD)] = (mixed / total).astype(BF16)
-            return carry
-
-        lax.fori_loop(0, GQ, one, 0)
+
+        each_head(one)
 
     def keys_near():
         arrived(keys_of(down), s.kr.at[down])
@@ -610,14 +618,15 @@
         0: [pass_query],
         2: [keys_near],
         3: [answer],
-        4: [second_queries],
-        6: [combine_z],
-        7: [keys_far, spread_rows],
-        8: [lambda: q_wait(3)],
-        9: [combine_y],
-        11: [pass_rows],
-        14: [rest_of_rows],
-        16: [far_rows],
+        4: [second_queries, lambda: spread_rows(1)],
+        5: [lambda: pass_rows(0)],
+        6: [combine_z, lambda: spread_rows(2)],
+        7: [keys_far, lambda: pass_rows(1)],
+        8: [lambda: q_wait(3), lambda: spread_rows(3)],
+        9: [combine_y, lambda: pass_rows(2)],
+        10: [lambda: pass_rows(3)],
+        12: [rest_of_rows],
+        14: [far_rows],
     }
 
     def prepare(i):
@@ -628,13 +637,13 @@
                 for action in todo:
                     action()
 
-        @pl.when(i >= 14)
+        @pl.when((i == 11) | ((i >= 13) & (i < 16)))
         def _():
-            join(i - 14)
-
-        @pl.when((i == 12) | (i >= 14))
+            join(jnp.maximum(i - 12, 0))
+
+        @pl.when((i == 10) | ((i >= 12) & (i < 15)))
         def _():
-            project(jnp.maximum(i - 13, 0))
+            project(jnp.maximum(i - 11, 0))
 
     def step(i, carry):
         scores_of(i, 1, s.ts1, s.mx1)
@@ -654,8 +663,6 @@
         action()
     scores_of(0, 0, s.ts0, s.mx0)
     lax.fori_loop(0, 16, step, 0)
-    join(RING - 1)
-
     for p in (1, 2, 3):
         arrived(s.orb.at[p], s.opr.at[p])
         arrived(s.lrb.at[p], s.lpr.at[p])
@@ -669,7 +676,7 @@
     for r in range(32):
         out_d[r] = total[r * STEPS : (r + 1) * STEPS, :].astype(BF16)
 
-    for copy in kv_own + kv_on + ay_own + ay_on:
+    for copy in kv_own + kv_on + [c for p in range(RING) for c in ay_own(p) + [ay_on(p)]]:
         copy.wait_send()
     for when, source, step_z, sem in q_first + q_second + q_third:
 

time: 77.8 us -> 76.8 us (0.987); the launches traced: 77.6 us -> 75.7 us
  Pallas kernels: 74.3 us -> 72.4 us
    pallas_call x1, Pallas kernels: 74.3 us -> 72.4 us  [shards(): pl.pallas_call(kernel, out_shape=(jax.ShapeDtypeStruct((SPAN, GQ * HD), B...]
where the time goes in v3:
time: 76.8 us; the launch traced here: 75.7 us
  Pallas kernels  72.4 us (94%)
  between operations  1.93 us (3%)
  local copies, waits for them, and re-layouts  1.36 us (2%)
    pallas_call x1, Pallas kernels, shards(): pl.pallas_call(kernel, out_shape=(jax.ShapeDtypeStruct((SPAN, GQ * HD), B...  72.4 us

profile of v3, /device:TPU:16, one launch (start us, length us, event | category | flops | bytes accessed | tf_op | source)
XLA Modules:
  0.0 75.7 jit_solution(12412612265863124697)
XLA Ops:
  1.9 72.4 %shard_map.113 = (bf16[128,1024]{1,0:T(8,128)(2,1)S(1)}, bf16[32,4,512]{2,1,0:T(4,128)(2,1)S(1)}) custom-call(s32[1]{0:T(128)S(6)} %copy.14.plen, s32[1]{0:T(128)S(6)} %copy.15.prow, s32[1,16]{1,0:T(1,128)} %clen_in.1, bf16[128,1024]{1,0:T(8,128)(2,1)} %bitcast.12, bf16[2,128,128]{2,1,0:T(8,128)(2,1)} %bitcast.14, bf16[2,896,128]{2,1,0:T(8,128)(2,1)} %bitcast.11, ...), custom_call_target="tpu_custom_call" | custom-call | flops 11000000512 | bytes 8000000 | tf_op jit(solution)/shard_map/pallas_call | solution.py:710
  74.3 0.7 copy.16
  75.0 0.7 copy.17

commit v4 on v3

--- a/solution.py
+++ b/solution.py
@@ -27,8 +27,8 @@
 BLOCK = 512
 VMEM_BYTES = 40 * 1024 * 1024
 
-PIECES = (0, 1, 1, 1, 2, 2, 2, 2, 3, 3, 3, 3, 1, 0, 0, 0)
-CHUNKS = (0, 0, 1, 2, 0, 1, 2, 3, 0, 1, 2, 3, 3, 1, 2, 3)
+PIECES = (0, 2, 2, 2, 2, 3, 3, 3, 3, 1, 1, 1, 1, 0, 0, 0)
+CHUNKS = (0, 0, 1, 2, 3, 0, 1, 2, 3, 0, 1, 2, 3, 1, 2, 3)
 
 
 def dot_nt(a, b):
@@ -305,11 +305,11 @@
         s.vn[pl.ds(r * STEPS, STEPS), :] = s.nkv[1, r].astype(F32)
 
     def picked(ref):
-        def add(r, total):
+        total = jnp.zeros((QROWS, HD), F32)
+        for r in range(ROWS):
             mine = jnp.where(me * ROWS + r == prow[0], 1.0, 0.0)
-            return total + mine * ref[pl.ds(pl.multiple_of(r * QROWS, QROWS), QROWS), :]
-
-        return lax.fori_loop(0, ROWS, add, jnp.zeros((QROWS, HD), F32))
+            total = total + mine * ref[r * QROWS : (r + 1) * QROWS, :]
+        return total
 
     s.sb[y] = picked(s.qf).astype(BF16)
 
@@ -348,15 +348,15 @@
         q_start(q_second)
 
     def some_rows(i, carry):
-        @pl.when(i == 2)
+        @pl.when(i == 1)
         def _():
             first_queries()
 
-        for u in range(4):
-            cached(i * 4 + u)
+        for u in range(8):
+            cached(i * 8 + u)
         return carry
 
-    lax.fori_loop(0, ROWS // 4, some_rows, 0)
+    lax.fori_loop(0, ROWS // 8, some_rows, 0)
     for h in range(GQ):
         s.ab[y, z, h] = s.of[pl.ds(h, ROWS * STEPS, stride=GQ), :].astype(BF16)
 
@@ -616,17 +616,17 @@
 
     actions = {
         0: [pass_query],
-        2: [keys_near],
-        3: [answer],
-        4: [second_queries, lambda: spread_rows(1)],
-        5: [lambda: pass_rows(0)],
-        6: [combine_z, lambda: spread_rows(2)],
-        7: [keys_far, lambda: pass_rows(1)],
-        8: [lambda: q_wait(3), lambda: spread_rows(3)],
-        9: [combine_y, lambda: pass_rows(2)],
-        10: [lambda: pass_rows(3)],
-        12: [rest_of_rows],
-        14: [far_rows],
+        1: [second_queries, keys_near],
+        2: [answer],
+        3: [lambda: spread_rows(1)],
+        4: [keys_far, lambda: pass_rows(0)],
+        5: [lambda: q_wait(3), lambda: spread_rows(2)],
+        6: [combine_z, lambda: pass_rows(1)],
+        7: [lambda: spread_rows(3)],
+        8: [combine_y, lambda: pass_rows(2)],
+        9: [lambda: pass_rows(3)],
+        11: [rest_of_rows],
+        13: [far_rows],
     }
 
     def prepare(i):
@@ -637,13 +637,13 @@
                 for action in todo:
                     action()
 
-        @pl.when((i == 11) | ((i >= 13) & (i < 16)))
-        def _():
-            join(jnp.maximum(i - 12, 0))
-
         @pl.when((i == 10) | ((i >= 12) & (i < 15)))
         def _():
-            project(jnp.maximum(i - 11, 0))
+            join(jnp.maximum(i - 11, 0))
+
+        @pl.when((i == 9) | ((i >= 11) & (i < 14)))
+        def _():
+            project(jnp.maximum(i - 10, 0))
 
     def step(i, carry):
         scores_of(i, 1, s.ts1, s.mx1)

time: 76.8 us -> 75.7 us (0.986); the launches traced: 75.7 us -> 75.5 us
  no operation moved by 1% of the time
where the time goes in v4:
time: 75.7 us; the launch traced here: 75.5 us
  Pallas kernels  72.2 us (95%)
  between operations  1.93 us (3%)
  local copies, waits for them, and re-layouts  1.36 us (2%)
    pallas_call x1, Pallas kernels, shards(): pl.pallas_call(kernel, out_shape=(jax.ShapeDtypeStruct((SPAN, GQ * HD), B...  72.2 us

profile of v4, /device:TPU:16, one launch (start us, length us, event | category | flops | bytes accessed | tf_op | source)
XLA Modules:
  0.0 75.5 jit_solution(3929428409942526439)
XLA Ops:
  1.9 72.2 %shard_map.113 = (bf16[128,1024]{1,0:T(8,128)(2,1)S(1)}, bf16[32,4,512]{2,1,0:T(4,128)(2,1)S(1)}) custom-call(s32[1]{0:T(128)S(6)} %copy.14.plen, s32[1]{0:T(128)S(6)} %copy.15.prow, s32[1,16]{1,0:T(1,128)} %clen_in.1, bf16[128,1024]{1,0:T(8,128)(2,1)} %bitcast.12, bf16[2,128,128]{2,1,0:T(8,128)(2,1)} %bitcast.14, bf16[2,896,128]{2,1,0:T(8,128)(2,1)} %bitcast.11, ...), custom_call_target="tpu_custom_call" | custom-call | flops 11000000512 | bytes 8000000 | tf_op jit(solution)/shard_map/pallas_call | solution.py:710
  74.2 0.7 copy.16
  74.9 0.7 copy.17

commit v5 on v4

--- a/solution.py
+++ b/solution.py
@@ -86,8 +86,10 @@
     "qb": pltpu.VMEM((RING, GQ * SPAN, HD), BF16),
     "ts0": pltpu.VMEM((BLOCK, KEYS), F32),
     "ts1": pltpu.VMEM((BLOCK, KEYS), F32),
-    "mx0": pltpu.VMEM((BLOCK, HD), F32),
-    "mx1": pltpu.VMEM((BLOCK, HD), F32),
+    "kp0": pltpu.VMEM((BLOCK, HD), F32),
+    "kp1": pltpu.VMEM((BLOCK, HD), F32),
+    "pk0": pltpu.VMEM((BLOCK, KEYS), BF16),
+    "pk1": pltpu.VMEM((BLOCK, KEYS), BF16),
     "dq": pltpu.VMEM((ROWS, STEPS, GQ * HD), BF16),
     "nkv": pltpu.VMEM((2, ROWS, STEPS, HD), BF16),
     "acc": pltpu.VMEM((RING, GQ * SPAN, HD), F32),
@@ -522,38 +524,64 @@
     first_lane = jnp.where(iota((BLOCK, HD), 1) == 0, 1.0, 0.0).astype(BF16)
     ones = jnp.ones((KEYS, HD), BF16)
 
-    def scores_of(at, b, held, peak):
+    def scores_of(at, b, held):
         p, yc = lookup(PIECES, at), turned(lookup(CHUNKS, at))
         zq = near(p)
-        late = (y * RING + zq) * SPAN - (yc * RING + z) * SPAN
-        shape = (SPAN, SPAN)
-        ahead = jnp.where(iota(shape, 1) - iota(shape, 0) <= late, 0.0, MASKED)
-        ahead = jnp.concatenate([ahead] * count, axis=0)
         queries = jnp.concatenate([s.qb[zq, b * BLOCK : (b + 1) * BLOCK, :], first_lane], axis=1)
-        scores = dot_nn(queries, s.kb[yc])
-        highest = None
-        for k in range(KEYS // HD):
-            cols = slice(k * HD, (k + 1) * HD)
-            part = scores[:, cols] * SCALE
-            if k == PRE // HD:
-                part = part + ahead
-            held[:, cols] = part
-            highest = part if highest is None else jnp.maximum(highest, part)
-        peak[...] = jnp.broadcast_to(jnp.max(highest, axis=1, keepdims=True), (BLOCK, HD))
-
-    def weigh(at, b, held, peak):
+
+        def quarter(j):
+            scores = dot_nn(queries, s.kb[yc, :, 2 * j * HD : 2 * (j + 1) * HD])
+            for k in (2 * j, 2 * j + 1):
+                part = scores[:, (k - 2 * j) * HD : (k - 2 * j + 1) * HD] * SCALE
+                if k == PRE // HD:
+                    late = (y * RING + zq) * SPAN - (yc * RING + z) * SPAN
+                    shape = (SPAN, SPAN)
+                    ahead = jnp.where(iota(shape, 1) - iota(shape, 0) <= late, 0.0, MASKED)
+                    part = part + jnp.concatenate([ahead] * count, axis=0)
+                held[:, k * HD : (k + 1) * HD] = part
+
+        return quarter
+
+    def weigh(at, b, held, keeps, packed):
+        p = lookup(PIECES, at)
+
+        def quarter(j):
+            for i in range(j * SPAN, (j + 1) * SPAN, 32):
+                mine = slice(i, i + 32)
+                rows = slice(b * BLOCK + i, b * BLOCK + i + 32)
+                tiles = [held[mine, k * HD : (k + 1) * HD] for k in range(KEYS // HD)]
+                highest = tiles[0]
+                for part in tiles[1:]:
+                    highest = jnp.maximum(highest, part)
+                before = s.top[p, rows, :]
+                after = jnp.maximum(before, jnp.max(highest, axis=1, keepdims=True))
+                s.top[p, rows, :] = after
+                keeps[mine, :] = jnp.exp2(before - after)
+                for k, part in enumerate(tiles):
+                    packed[mine, k * HD : (k + 1) * HD] = jnp.exp2(part - after).astype(BF16)
+
+        return quarter
+
+    def mix(at, b, keeps, packed):
         p, yc = lookup(PIECES, at), turned(lookup(CHUNKS, at))
-        rows = slice(b * BLOCK, (b + 1) * BLOCK)
-        before = s.top[p, rows, :]
-        after = jnp.maximum(before, peak[...])
-        keep = jnp.exp2(before - after)
-        packed = []
-        for k in range(KEYS // HD):
-            packed.append(jnp.exp2(held[:, k * HD : (k + 1) * HD] - after).astype(BF16))
-        mixed = dot_nn(jnp.concatenate(packed, axis=1), jnp.concatenate([s.vb[yc], ones], axis=1))
-        s.top[p, rows, :] = after
-        s.tot[p, rows, :] = s.tot[p, rows, :] * keep + mixed[:, HD:]
-        s.acc[p, rows, :] = s.acc[p, rows, :] * keep + mixed[:, :HD]
+
+        def half_block(j):
+            size = BLOCK // 2
+            mine = slice(j * size, (j + 1) * size)
+            rows = slice(b * BLOCK + j * size, b * BLOCK + (j + 1) * size)
+            mixed = dot_nn(packed[mine, :], jnp.concatenate([s.vb[yc], ones], axis=1))
+            keep = keeps[mine, :]
+            s.tot[p, rows, :] = s.tot[p, rows, :] * keep + mixed[:, HD:]
+            s.acc[p, rows, :] = s.acc[p, rows, :] * keep + mixed[:, :HD]
+
+        return half_block
+
+    def together(scores, weights, products):
+        for j in range(4):
+            scores(j)
+            weights(j)
+            if j % 2 == 0:
+                products(j // 2)
 
     def o_copies(p):
         return [
@@ -645,24 +673,34 @@
         def _():
             project(jnp.maximum(i - 10, 0))
 
+    even = (s.ts0, s.kp0, s.pk0)
+    odd = (s.ts1, s.kp1, s.pk1)
+
     def step(i, carry):
-        scores_of(i, 1, s.ts1, s.mx1)
-        weigh(i, 0, s.ts0, s.mx0)
-        prepare(i + 1)
-        scores_of(jnp.minimum(i + 1, 15), 0, s.ts0, s.mx0)
-        weigh(i, 1, s.ts1, s.mx1)
-        p, k = lookup(PIECES, i), lookup(CHUNKS, i)
+        last = jnp.maximum(i - 1, 0)
+        together(scores_of(i, 1, odd[0]), weigh(i, 0, *even), mix(last, 1, *odd[1:]))
+        p, k = lookup(PIECES, last), lookup(CHUNKS, last)
 
         @pl.when((k == 3) & (p > 0))
         def _():
             ship(p)
 
+        prepare(i + 1)
+        together(scores_of(jnp.minimum(i + 1, 15), 0, even[0]), weigh(i, 1, *odd), mix(i, 0, *even[1:]))
         return carry
 
+    s.kp1[...] = jnp.ones((BLOCK, HD), F32)
+    s.pk1[...] = jnp.zeros((BLOCK, KEYS), BF16)
     for action in actions.pop(0):
         action()
-    scores_of(0, 0, s.ts0, s.mx0)
+    first = scores_of(0, 0, s.ts0)
+    for j in range(4):
+        first(j)
     lax.fori_loop(0, 16, step, 0)
+    rest = mix(15, 1, *odd[1:])
+    for j in range(2):
+        rest(j)
+
     for p in (1, 2, 3):
         arrived(s.orb.at[p], s.opr.at[p])
         arrived(s.lrb.at[p], s.lpr.at[p])

time: 75.7 us -> 78 us (1.030); the launches traced: 75.5 us -> 77 us
  Pallas kernels: 72.2 us -> 73.7 us
    pallas_call x1, Pallas kernels: 72.2 us -> 73.7 us  [shards(): pl.pallas_call(kernel, out_shape=(jax.ShapeDtypeStruct((SPAN, GQ * HD), B...]
where the time goes in v5:
time: 78 us; the launch traced here: 77 us
  Pallas kernels  73.7 us (94%)
  between operations  1.93 us (2%)
  local copies, waits for them, and re-layouts  1.36 us (2%)
    pallas_call x1, Pallas kernels, shards(): pl.pallas_call(kernel, out_shape=(jax.ShapeDtypeStruct((SPAN, GQ * HD), B...  73.7 us

profile of v5, /device:TPU:16, one launch (start us, length us, event | category | flops | bytes accessed | tf_op | source)
XLA Modules:
  0.0 77.0 jit_solution(17513324399920259111)
XLA Ops:
  1.9 73.7 %shard_map.113 = (bf16[128,1024]{1,0:T(8,128)(2,1)S(1)}, bf16[32,4,512]{2,1,0:T(4,128)(2,1)S(1)}) custom-call(s32[1]{0:T(128)S(6)} %copy.14.plen, s32[1]{0:T(128)S(6)} %copy.15.prow, s32[1,16]{1,0:T(1,128)} %clen_in.1, bf16[128,1024]{1,0:T(8,128)(2,1)} %bitcast.12, bf16[2,128,128]{2,1,0:T(8,128)(2,1)} %bitcast.14, bf16[2,896,128]{2,1,0:T(8,128)(2,1)} %bitcast.11, ...), custom_call_target="tpu_custom_call" | custom-call | flops 11000000512 | bytes 8000000 | tf_op jit(solution)/shard_map/pallas_call | solution.py:748
  75.6 0.7 copy.16
  76.3 0.7 copy.17

commit v6 on v4

--- a/solution.py
+++ b/solution.py
@@ -24,8 +24,8 @@
 MESH = pl.DeviceIdType.MESH
 F32 = jnp.float32
 BF16 = jnp.bfloat16
-BLOCK = 512
-VMEM_BYTES = 40 * 1024 * 1024
+BLOCK = GQ * SPAN
+VMEM_BYTES = 52 * 1024 * 1024
 
 PIECES = (0, 2, 2, 2, 2, 3, 3, 3, 3, 1, 1, 1, 1, 0, 0, 0)
 CHUNKS = (0, 0, 1, 2, 3, 0, 1, 2, 3, 0, 1, 2, 3, 1, 2, 3)
@@ -86,8 +86,9 @@
     "qb": pltpu.VMEM((RING, GQ * SPAN, HD), BF16),
     "ts0": pltpu.VMEM((BLOCK, KEYS), F32),
     "ts1": pltpu.VMEM((BLOCK, KEYS), F32),
-    "mx0": pltpu.VMEM((BLOCK, HD), F32),
-    "mx1": pltpu.VMEM((BLOCK, HD), F32),
+    "kp": pltpu.VMEM((BLOCK, HD), F32),
+    "pk": pltpu.VMEM((BLOCK, KEYS), BF16),
+    "ahead": pltpu.VMEM((SPAN, SPAN), F32),
     "dq": pltpu.VMEM((ROWS, STEPS, GQ * HD), BF16),
     "nkv": pltpu.VMEM((2, ROWS, STEPS, HD), BF16),
     "acc": pltpu.VMEM((RING, GQ * SPAN, HD), F32),
@@ -518,42 +519,51 @@
             s.xo[j] = total.astype(BF16)
             xi_copy(j).start()
 
-    count = BLOCK // SPAN
     first_lane = jnp.where(iota((BLOCK, HD), 1) == 0, 1.0, 0.0).astype(BF16)
     ones = jnp.ones((KEYS, HD), BF16)
 
-    def scores_of(at, b, held, peak):
+    def scores_of(at, held):
         p, yc = lookup(PIECES, at), turned(lookup(CHUNKS, at))
-        zq = near(p)
-        late = (y * RING + zq) * SPAN - (yc * RING + z) * SPAN
+        queries = jnp.concatenate([s.qb[near(p)], first_lane], axis=1)
+
+        def quarter(j):
+            cols = slice(j * KEYS // 4, (j + 1) * KEYS // 4)
+            held[:, cols] = dot_nn(queries, s.kb[yc, :, cols])
+
+        return quarter
+
+    def weigh(at, held):
+        p, yc = lookup(PIECES, at), turned(lookup(CHUNKS, at))
+        late = (y * RING + near(p)) * SPAN - (yc * RING + z) * SPAN
         shape = (SPAN, SPAN)
-        ahead = jnp.where(iota(shape, 1) - iota(shape, 0) <= late, 0.0, MASKED)
-        ahead = jnp.concatenate([ahead] * count, axis=0)
-        queries = jnp.concatenate([s.qb[zq, b * BLOCK : (b + 1) * BLOCK, :], first_lane], axis=1)
-        scores = dot_nn(queries, s.kb[yc])
-        highest = None
-        for k in range(KEYS // HD):
-            cols = slice(k * HD, (k + 1) * HD)
-            part = scores[:, cols] * SCALE
-            if k == PRE // HD:
-                part = part + ahead
-            held[:, cols] = part
-            highest = part if highest is None else jnp.maximum(highest, part)
-        peak[...] = jnp.broadcast_to(jnp.max(highest, axis=1, keepdims=True), (BLOCK, HD))
-
-    def weigh(at, b, held, peak):
+        s.ahead[...] = jnp.where(iota(shape, 1) - iota(shape, 0) <= late, 0.0, MASKED)
+
+        def quarter(j):
+            for i in range(j * BLOCK // 4, (j + 1) * BLOCK // 4, 32):
+                rows = slice(i, i + 32)
+                tiles = [held[rows, k * HD : (k + 1) * HD] for k in range(KEYS // HD)]
+                tiles[-1] = tiles[-1] + s.ahead[i % SPAN : i % SPAN + 32, :]
+                highest = tiles[0]
+                for part in tiles[1:]:
+                    highest = jnp.maximum(highest, part)
+                before = s.top[p, rows, :]
+                after = jnp.maximum(before, jnp.max(highest, axis=1, keepdims=True))
+                s.top[p, rows, :] = after
+                s.kp[rows, :] = jnp.exp2((before - after) * SCALE)
+                for k, part in enumerate(tiles):
+                    s.pk[rows, k * HD : (k + 1) * HD] = jnp.exp2((part - after) * SCALE).astype(BF16)
+
+        return quarter
+
+    def mix(at):
         p, yc = lookup(PIECES, at), turned(lookup(CHUNKS, at))
-        rows = slice(b * BLOCK, (b + 1) * BLOCK)
-        before = s.top[p, rows, :]
-        after = jnp.maximum(before, peak[...])
-        keep = jnp.exp2(before - after)
-        packed = []
-        for k in range(KEYS // HD):
-            packed.append(jnp.exp2(held[:, k * HD : (k + 1) * HD] - after).astype(BF16))
-        mixed = dot_nn(jnp.concatenate(packed, axis=1), jnp.concatenate([s.vb[yc], ones], axis=1))
-        s.top[p, rows, :] = after
-        s.tot[p, rows, :] = s.tot[p, rows, :] * keep + mixed[:, HD:]
-        s.acc[p, rows, :] = s.acc[p, rows, :] * keep + mixed[:, :HD]
+        mixed = dot_nn(s.pk[...], jnp.concatenate([s.vb[yc], ones], axis=1))
+        s.tot[p] = s.tot[p] * s.kp[...] + mixed[:, HD:]
+        s.acc[p] = s.acc[p] * s.kp[...] + mixed[:, :HD]
+
+        @pl.when((lookup(CHUNKS, at) == 3) & (p > 0))
+        def _():
+            ship(p)
 
     def o_copies(p):
         return [
@@ -574,7 +584,7 @@
             rows = pl.ds(pl.multiple_of(h * SPAN, SPAN), SPAN)
             total = s.tot[p, rows, :]
             s.os[p, h] = (s.acc[p, rows, :] / total).astype(BF16)
-            s.ls[p, pl.ds(h, 1), :] = to_row(s.top[p, rows, :] + log2(total))
+            s.ls[p, pl.ds(h, 1), :] = to_row(s.top[p, rows, :] * SCALE + log2(total))
 
         each_head(one)
         for copy in o_copies(p):
@@ -584,10 +594,11 @@
         def one(h):
             rows = pl.ds(pl.multiple_of(h * SPAN, SPAN), SPAN)
             levels = [to_column(s.lrb[p, pl.ds(h, 1), :], SPAN) for p in (1, 2, 3)]
-            top = s.top[0, rows, :]
+            own = s.top[0, rows, :] * SCALE
+            top = own
             for level in levels:
                 top = jnp.maximum(top, level)
-            weight = jnp.exp2(s.top[0, rows, :] - top)
+            weight = jnp.exp2(own - top)
             total = s.tot[0, rows, :] * weight
             mixed = s.acc[0, rows, :] * weight
             for p, level in zip((1, 2, 3), levels):
@@ -629,8 +640,10 @@
         13: [far_rows],
     }
 
-    def prepare(i):
+    def prepare(i, parity):
         for at, todo in actions.items():
+            if at % 2 != parity:
+                continue
 
             @pl.when(i == at)
             def _(todo=todo):
@@ -645,24 +658,26 @@
         def _():
             project(jnp.maximum(i - 10, 0))
 
+    def unit(i, parity, held, later):
+        prepare(i + 1, 1 - parity)
+        scores, weights = scores_of(jnp.minimum(i + 1, 15), later), weigh(i, held)
+        for j in range(4):
+            scores(j)
+            weights(j)
+        mix(i)
+
     def step(i, carry):
-        scores_of(i, 1, s.ts1, s.mx1)
-        weigh(i, 0, s.ts0, s.mx0)
-        prepare(i + 1)
-        scores_of(jnp.minimum(i + 1, 15), 0, s.ts0, s.mx0)
-        weigh(i, 1, s.ts1, s.mx1)
-        p, k = lookup(PIECES, i), lookup(CHUNKS, i)
-
-        @pl.when((k == 3) & (p > 0))
-        def _():
-            ship(p)
-
+        unit(2 * i, 0, s.ts0, s.ts1)
+        unit(2 * i + 1, 1, s.ts1, s.ts0)
         return carry
 
     for action in actions.pop(0):
         action()
-    scores_of(0, 0, s.ts0, s.mx0)
-    lax.fori_loop(0, 16, step, 0)
+    first = scores_of(0, s.ts0)
+    for j in range(4):
+        first(j)
+    lax.fori_loop(0, 8, step, 0)
+
     for p in (1, 2, 3):
         arrived(s.orb.at[p], s.opr.at[p])
         arrived(s.lrb.at[p], s.lpr.at[p])

time: 75.7 us -> 75.4 us (level); the launches traced: 75.5 us -> 74.2 us
  Pallas kernels: 72.2 us -> 70.9 us
    pallas_call x1, Pallas kernels: 72.2 us -> 70.9 us  [shards(): pl.pallas_call(kernel, out_shape=(jax.ShapeDtypeStruct((SPAN, GQ * HD), B...]
where the time goes in v6:
time: 75.4 us; the launch traced here: 74.2 us
  Pallas kernels  70.9 us (94%)
  between operations  1.93 us (3%)
  local copies, waits for them, and re-layouts  1.36 us (2%)
    pallas_call x1, Pallas kernels, shards(): pl.pallas_call(kernel, out_shape=(jax.ShapeDtypeStruct((SPAN, GQ * HD), B...  70.9 us

profile of v6, /device:TPU:16, one launch (start us, length us, event | category | flops | bytes accessed | tf_op | source)
XLA Modules:
  0.0 74.2 jit_solution(4032139285842654656)
XLA Ops:
  1.9 70.9 %shard_map.113 = (bf16[128,1024]{1,0:T(8,128)(2,1)S(1)}, bf16[32,4,512]{2,1,0:T(4,128)(2,1)S(1)}) custom-call(s32[1]{0:T(128)S(6)} %copy.14.plen, s32[1]{0:T(128)S(6)} %copy.15.prow, s32[1,16]{1,0:T(1,128)} %clen_in.1, bf16[128,1024]{1,0:T(8,128)(2,1)} %bitcast.12, bf16[2,128,128]{2,1,0:T(8,128)(2,1)} %bitcast.14, bf16[2,896,128]{2,1,0:T(8,128)(2,1)} %bitcast.11, ...), custom_call_target="tpu_custom_call" | custom-call | flops 11000000512 | bytes 8000000 | tf_op jit(solution)/shard_map/pallas_call | solution.py:725
  72.9 0.7 copy.16
  73.6 0.7 copy.17

commit v7 on v4

--- a/solution.py
+++ b/solution.py
@@ -27,8 +27,8 @@
 BLOCK = 512
 VMEM_BYTES = 40 * 1024 * 1024
 
-PIECES = (0, 2, 2, 2, 2, 3, 3, 3, 3, 1, 1, 1, 1, 0, 0, 0)
-CHUNKS = (0, 0, 1, 2, 3, 0, 1, 2, 3, 0, 1, 2, 3, 1, 2, 3)
+PIECES = (0, 1, 1, 1, 2, 2, 2, 2, 1, 3, 3, 3, 3, 0, 0, 0)
+CHUNKS = (0, 0, 1, 2, 0, 1, 2, 3, 3, 0, 1, 2, 3, 1, 2, 3)
 
 
 def dot_nt(a, b):
@@ -148,7 +148,7 @@
     "h2r": pltpu.SemaphoreType.DMA((RING,)),
     "hl2s": pltpu.SemaphoreType.DMA((RING,)),
     "hl2r": pltpu.SemaphoreType.DMA((RING,)),
-    "as_": pltpu.SemaphoreType.DMA((RING,)),
+    "as_": pltpu.SemaphoreType.DMA((6,)),
     "ar": pltpu.SemaphoreType.DMA((RING,)),
     "ays": pltpu.SemaphoreType.DMA((3 * RING,)),
     "ayr": pltpu.SemaphoreType.DMA((RING, RING)),
@@ -260,32 +260,42 @@
     def q_copy(source, step, sem):
         return send(s.qb.at[source], s.qb.at[source], s.qs.at[sem], s.qr.at[source], at_z(z + step))
 
+    def a_copy(source, step, sem):
+        block = s.ab.at[y, source]
+        return send(block, block, s.as_.at[sem], s.ar.at[source], at_z(z + step))
+
     q_first = [(z < 3, z, 1, 0), (z > 0, z, -1, 1)]
     q_second = [((z > 0) & (z < 3), z - 1, 1, 2), ((z > 0) & (z < 3), z + 1, -1, 3)]
     q_third = [(z == 2, z - 2, 1, 4), (z == 1, z + 2, -1, 5)]
 
-    def q_start(group):
+    def z_start(copy, group):
         for when, source, step, sem in group:
 
             @pl.when(when)
             def _(source=source, step=step, sem=sem):
-                q_copy(source, step, sem).start()
-
-    def q_wait(distance):
+                copy(source, step, sem).start()
+
+    def z_wait(block, sems, distance):
         @pl.when(z >= distance)
         def _():
-            arrived(s.qb.at[z - distance], s.qr.at[z - distance])
+            arrived(block(z - distance), sems.at[z - distance])
 
         @pl.when(z + distance < RING)
         def _():
-            arrived(s.qb.at[z + distance], s.qr.at[z + distance])
+            arrived(block(z + distance), sems.at[z + distance])
+
+    def q_wait(distance):
+        z_wait(lambda source: s.qb.at[source], s.qr, distance)
+
+    def a_wait(distance):
+        z_wait(lambda source: s.ab.at[y, source], s.ar, distance)
 
     def b_copy(d):
         return send(s.sb.at[y], s.sb.at[y], s.bs.at[d], s.br.at[y], at_y(lax.rem(y + d, RING)))
 
     for copy in kv_own[:2]:
         copy.start()
-    q_start(q_first)
+    z_start(q_copy, q_first)
     for load in loads[:2]:
         load.wait()
     s.kb[y, 0:HD, :] = s.kl[...].T
@@ -345,12 +355,14 @@
 
     def first_queries():
         q_wait(1)
-        q_start(q_second)
+        z_start(q_copy, q_second)
 
     def some_rows(i, carry):
         @pl.when(i == 1)
         def _():
             first_queries()
+            arrived(s.vb.at[up], s.vr.at[up])
+            kv_on[1].start()
 
         for u in range(8):
             cached(i * 8 + u)
@@ -360,9 +372,6 @@
     for h in range(GQ):
         s.ab[y, z, h] = s.of[pl.ds(h, ROWS * STEPS, stride=GQ), :].astype(BF16)
 
-    def a_copy(p):
-        return send(s.ab.at[y, z], s.ab.at[y, z], s.as_.at[p], s.ar.at[z], at_z(near(p)))
-
     def ay_copy(yy, p, sem, to):
         block = s.ab.at[yy, near(p)]
         return send(block, block, s.ays.at[sem], s.ayr.at[yy, near(p)], at_y(to))
@@ -378,7 +387,8 @@
 
     def spread_rows(p):
         if p:
-            arrived(s.ab.at[y, near(p)], s.ar.at[near(p)])
+            a_wait(p)
+            z_start(a_copy, (q_second, q_third, [])[p - 1])
         for copy in ay_own(p):
             copy.start()
 
@@ -394,8 +404,7 @@
         for p in range(RING):
             rows_in(far, p)
 
-    for p in (1, 2, 3):
-        a_copy(p).start()
+    z_start(a_copy, q_first)
     spread_rows(0)
     s.sl[z] = jnp.broadcast_to(to_row(picked(s.lf)), (8, HD))
 
@@ -598,11 +607,11 @@
 
         each_head(one)
 
-    def keys_near():
+    def pass_keys():
         arrived(keys_of(down), s.kr.at[down])
         kv_on[0].start()
-        arrived(s.vb.at[up], s.vr.at[up])
-        kv_on[1].start()
+
+    def keys_near():
         arrived(s.vb.at[down], s.vr.at[down])
         arrived(keys_of(up), s.kr.at[up])
 
@@ -612,21 +621,23 @@
 
     def second_queries():
         q_wait(2)
-        q_start(q_third)
+        z_start(q_copy, q_third)
 
     actions = {
         0: [pass_query],
-        1: [second_queries, keys_near],
-        2: [answer],
-        3: [lambda: spread_rows(1)],
-        4: [keys_far, lambda: pass_rows(0)],
-        5: [lambda: q_wait(3), lambda: spread_rows(2)],
-        6: [combine_z, lambda: pass_rows(1)],
-        7: [lambda: spread_rows(3)],
-        8: [combine_y, lambda: pass_rows(2)],
-        9: [lambda: pass_rows(3)],
-        11: [rest_of_rows],
-        13: [far_rows],
+        1: [pass_keys],
+        2: [keys_near],
+        3: [second_queries, lambda: spread_rows(1)],
+        4: [answer],
+        5: [lambda: spread_rows(2), lambda: pass_rows(0)],
+        6: [combine_z],
+        7: [keys_far, lambda: pass_rows(1)],
+        8: [lambda: spread_rows(3)],
+        9: [lambda: q_wait(3)],
+        10: [combine_y, lambda: pass_rows(2)],
+        11: [lambda: pass_rows(3)],
+        14: [rest_of_rows],
+        16: [far_rows],
     }
 
     def prepare(i):
@@ -637,13 +648,13 @@
                 for action in todo:
                     action()
 
-        @pl.when((i == 10) | ((i >= 12) & (i < 15)))
+        @pl.when((i == 12) | (i >= 15))
         def _():
-            join(jnp.maximum(i - 11, 0))
-
-        @pl.when((i == 9) | ((i >= 11) & (i < 14)))
+            join(jnp.maximum(i - 14, 0))
+
+        @pl.when((i == 11) | (i >= 14))
         def _():
-            project(jnp.maximum(i - 10, 0))
+            project(jnp.maximum(i - 13, 0))
 
     def step(i, carry):
         scores_of(i, 1, s.ts1, s.mx1)
@@ -663,6 +674,7 @@
         action()
     scores_of(0, 0, s.ts0, s.mx0)
     lax.fori_loop(0, 16, step, 0)
+    join(RING - 1)
     for p in (1, 2, 3):
         arrived(s.orb.at[p], s.opr.at[p])
         arrived(s.lrb.at[p], s.lpr.at[p])
@@ -683,6 +695,7 @@
         @pl.when(when)
         def _(source=source, step_z=step_z, sem=sem):
             q_copy(source, step_z, sem).wait_send()
+            a_copy(source, step_z, sem).wait_send()
 
     for d in range(RING):
         x_copy(d).wait_send()
@@ -690,7 +703,6 @@
             copy.wait_send()
         if d:
             b_copy(d).wait_send()
-            a_copy(d).wait_send()
             for copy in h2_copies(d):
                 copy.wait_send()
             for copy in o_copies(d):

time: 75.7 us -> 75.9 us (level)
  no operation moved by 1% of the time
where the time goes in v7:
time: 75.9 us; the launch traced here: 75.7 us
  Pallas kernels  72.4 us (95%)
  between operations  1.93 us (3%)
  local copies, waits for them, and re-layouts  1.36 us (2%)
    pallas_call x1, Pallas kernels, shards(): pl.pallas_call(kernel, out_shape=(jax.ShapeDtypeStruct((SPAN, GQ * HD), B...  72.4 us

profile of v7, /device:TPU:16, one launch (start us, length us, event | category | flops | bytes accessed | tf_op | source)
XLA Modules:
  0.0 75.7 jit_solution(8350724870000586274)
XLA Ops:
  1.9 72.4 %shard_map.113 = (bf16[128,1024]{1,0:T(8,128)(2,1)S(1)}, bf16[32,4,512]{2,1,0:T(4,128)(2,1)S(1)}) custom-call(s32[1]{0:T(128)S(6)} %copy.14.plen, s32[1]{0:T(128)S(6)} %copy.15.prow, s32[1,16]{1,0:T(1,128)} %clen_in.1, bf16[128,1024]{1,0:T(8,128)(2,1)} %bitcast.12, bf16[2,128,128]{2,1,0:T(8,128)(2,1)} %bitcast.14, bf16[2,896,128]{2,1,0:T(8,128)(2,1)} %bitcast.11, ...), custom_call_target="tpu_custom_call" | custom-call | flops 11000000512 | bytes 8000000 | tf_op jit(solution)/shard_map/pallas_call | solution.py:722
  74.3 0.7 copy.16
  75.0 0.7 copy.17

commit v8 on v7

--- a/solution.py
+++ b/solution.py
@@ -27,8 +27,8 @@
 BLOCK = 512
 VMEM_BYTES = 40 * 1024 * 1024
 
-PIECES = (0, 1, 1, 1, 2, 2, 2, 2, 1, 3, 3, 3, 3, 0, 0, 0)
-CHUNKS = (0, 0, 1, 2, 0, 1, 2, 3, 3, 0, 1, 2, 3, 1, 2, 3)
+PIECES = (0, 2, 2, 2, 2, 3, 3, 3, 3, 1, 1, 1, 1, 0, 0, 0)
+CHUNKS = (0, 0, 1, 2, 3, 0, 1, 2, 3, 0, 1, 2, 3, 1, 2, 3)
 
 
 def dot_nt(a, b):
@@ -625,18 +625,16 @@
 
     actions = {
         0: [pass_query],
-        1: [pass_keys],
+        1: [second_queries, pass_keys],
         2: [keys_near],
-        3: [second_queries, lambda: spread_rows(1)],
-        4: [answer],
-        5: [lambda: spread_rows(2), lambda: pass_rows(0)],
-        6: [combine_z],
-        7: [keys_far, lambda: pass_rows(1)],
-        8: [lambda: spread_rows(3)],
-        9: [lambda: q_wait(3)],
-        10: [combine_y, lambda: pass_rows(2)],
-        11: [lambda: pass_rows(3)],
-        14: [rest_of_rows],
+        3: [lambda: spread_rows(1), answer],
+        4: [keys_far, lambda: pass_rows(0)],
+        5: [lambda: q_wait(3), lambda: spread_rows(2)],
+        6: [combine_z, lambda: pass_rows(1)],
+        7: [lambda: spread_rows(3)],
+        8: [combine_y, lambda: pass_rows(2)],
+        9: [lambda: pass_rows(3)],
+        13: [rest_of_rows],
         16: [far_rows],
     }
 
@@ -648,13 +646,13 @@
                 for action in todo:
                     action()
 
-        @pl.when((i == 12) | (i >= 15))
+        @pl.when((i == 10) | (i == 14) | (i == 16))
         def _():
-            join(jnp.maximum(i - 14, 0))
-
-        @pl.when((i == 11) | (i >= 14))
+            join(lax.div(jnp.maximum(i - 12, 0), 2))
+
+        @pl.when((i == 9) | (i == 13) | (i == 14) | (i == 16))
         def _():
-            project(jnp.maximum(i - 13, 0))
+            project(jnp.minimum(jnp.maximum(i - 12, 0), 3))
 
     def step(i, carry):
         scores_of(i, 1, s.ts1, s.mx1)

time: 75.9 us -> 80.3 us (1.058)
  Pallas kernels: 72.4 us -> 76.8 us
    pallas_call x1, Pallas kernels: 72.4 us -> 76.8 us  [shards(): pl.pallas_call(kernel, out_shape=(jax.ShapeDtypeStruct((SPAN, GQ * HD), B...]
where the time goes in v8:
time: 80.3 us; the launch traced here: 80.1 us
  Pallas kernels  76.8 us (96%)
  between operations  1.93 us (2%)
  local copies, waits for them, and re-layouts  1.36 us (2%)
    pallas_call x1, Pallas kernels, shards(): pl.pallas_call(kernel, out_shape=(jax.ShapeDtypeStruct((SPAN, GQ * HD), B...  76.8 us

profile of v8, /device:TPU:16, one launch (start us, length us, event | category | flops | bytes accessed | tf_op | source)
XLA Modules:
  0.0 80.1 jit_solution(18426690721903249979)
XLA Ops:
  1.9 76.8 %shard_map.113 = (bf16[128,1024]{1,0:T(8,128)(2,1)S(1)}, bf16[32,4,512]{2,1,0:T(4,128)(2,1)S(1)}) custom-call(s32[1]{0:T(128)S(6)} %copy.14.plen, s32[1]{0:T(128)S(6)} %copy.15.prow, s32[1,16]{1,0:T(1,128)} %clen_in.1, bf16[128,1024]{1,0:T(8,128)(2,1)} %bitcast.12, bf16[2,128,128]{2,1,0:T(8,128)(2,1)} %bitcast.14, bf16[2,896,128]{2,1,0:T(8,128)(2,1)} %bitcast.11, ...), custom_call_target="tpu_custom_call" | custom-call | flops 11000000512 | bytes 8000000 | tf_op jit(solution)/shard_map/pallas_call | solution.py:720
  78.7 0.7 copy.16
  79.4 0.7 copy.17

commit v9 on v7

--- a/solution.py
+++ b/solution.py
@@ -27,8 +27,8 @@
 BLOCK = 512
 VMEM_BYTES = 40 * 1024 * 1024
 
-PIECES = (0, 1, 1, 1, 2, 2, 2, 2, 1, 3, 3, 3, 3, 0, 0, 0)
-CHUNKS = (0, 0, 1, 2, 0, 1, 2, 3, 3, 0, 1, 2, 3, 1, 2, 3)
+PIECES = (0, 1, 2, 2, 2, 2, 3, 3, 3, 3, 1, 1, 1, 0, 0, 0)
+CHUNKS = (0, 0, 0, 1, 2, 3, 0, 1, 2, 3, 1, 2, 3, 1, 2, 3)
 
 
 def dot_nt(a, b):
@@ -358,12 +358,6 @@
         z_start(q_copy, q_second)
 
     def some_rows(i, carry):
-        @pl.when(i == 1)
-        def _():
-            first_queries()
-            arrived(s.vb.at[up], s.vr.at[up])
-            kv_on[1].start()
-
         for u in range(8):
             cached(i * 8 + u)
         return carry
@@ -607,6 +601,10 @@
 
         each_head(one)
 
+    def pass_values():
+        arrived(s.vb.at[up], s.vr.at[up])
+        kv_on[1].start()
+
     def pass_keys():
         arrived(keys_of(down), s.kr.at[down])
         kv_on[0].start()
@@ -624,20 +622,18 @@
         z_start(q_copy, q_third)
 
     actions = {
-        0: [pass_query],
-        1: [pass_keys],
-        2: [keys_near],
-        3: [second_queries, lambda: spread_rows(1)],
+        1: [first_queries, pass_values],
+        2: [pass_keys, second_queries, pass_query],
+        3: [keys_near, lambda: spread_rows(1)],
         4: [answer],
-        5: [lambda: spread_rows(2), lambda: pass_rows(0)],
-        6: [combine_z],
-        7: [keys_far, lambda: pass_rows(1)],
+        5: [keys_far, lambda: pass_rows(0)],
+        6: [lambda: q_wait(3), lambda: spread_rows(2)],
+        7: [combine_z, lambda: pass_rows(1)],
         8: [lambda: spread_rows(3)],
-        9: [lambda: q_wait(3)],
-        10: [combine_y, lambda: pass_rows(2)],
-        11: [lambda: pass_rows(3)],
-        14: [rest_of_rows],
-        16: [far_rows],
+        9: [combine_y, lambda: pass_rows(2)],
+        10: [lambda: pass_rows(3)],
+        12: [rest_of_rows],
+        14: [far_rows],
     }
 
     def prepare(i):
@@ -648,13 +644,13 @@
                 for action in todo:
                     action()
 
-        @pl.when((i == 12) | (i >= 15))
+        @pl.when((i == 11) | ((i >= 13) & (i < 16)))
         def _():
-            join(jnp.maximum(i - 14, 0))
-
-        @pl.when((i == 11) | (i >= 14))
+            join(jnp.maximum(i - 12, 0))
+
+        @pl.when((i == 10) | ((i >= 12) & (i < 15)))
         def _():
-            project(jnp.maximum(i - 13, 0))
+            project(jnp.maximum(i - 11, 0))
 
     def step(i, carry):
         scores_of(i, 1, s.ts1, s.mx1)
@@ -670,11 +666,8 @@
 
         return carry
 
-    for action in actions.pop(0):
-        action()
     scores_of(0, 0, s.ts0, s.mx0)
     lax.fori_loop(0, 16, step, 0)
-    join(RING - 1)
     for p in (1, 2, 3):
         arrived(s.orb.at[p], s.opr.at[p])
         arrived(s.lrb.at[p], s.lpr.at[p])

time: 75.9 us -> 72.5 us (0.955)
  Pallas kernels: 72.4 us -> 69.1 us
    pallas_call x1, Pallas kernels: 72.4 us -> 69.1 us  [shards(): pl.pallas_call(kernel, out_shape=(jax.ShapeDtypeStruct((SPAN, GQ * HD), B...]
where the time goes in v9:
time: 72.5 us; the launch traced here: 72.3 us
  Pallas kernels  69.1 us (95%)
  between operations  1.93 us (3%)
  local copies, waits for them, and re-layouts  1.36 us (2%)
    pallas_call x1, Pallas kernels, shards(): pl.pallas_call(kernel, out_shape=(jax.ShapeDtypeStruct((SPAN, GQ * HD), B...  69.1 us

profile of v9, /device:TPU:16, one launch (start us, length us, event | category | flops | bytes accessed | tf_op | source)
XLA Modules:
  0.0 72.3 jit_solution(16545071815134174120)
XLA Ops:
  1.9 69.1 %shard_map.113 = (bf16[128,1024]{1,0:T(8,128)(2,1)S(1)}, bf16[32,4,512]{2,1,0:T(4,128)(2,1)S(1)}) custom-call(s32[1]{0:T(128)S(6)} %copy.14.plen, s32[1]{0:T(128)S(6)} %copy.15.prow, s32[1,16]{1,0:T(1,128)} %clen_in.1, bf16[128,1024]{1,0:T(8,128)(2,1)} %bitcast.12, bf16[2,128,128]{2,1,0:T(8,128)(2,1)} %bitcast.14, bf16[2,896,128]{2,1,0:T(8,128)(2,1)} %bitcast.11, ...), custom_call_target="tpu_custom_call" | custom-call | flops 11000000512 | bytes 8000000 | tf_op jit(solution)/shard_map/pallas_call | solution.py:715
  71.0 0.7 copy.16
  71.7 0.7 copy.17

commit v10 on v9

--- a/solution.py
+++ b/solution.py
@@ -27,8 +27,12 @@
 BLOCK = 512
 VMEM_BYTES = 40 * 1024 * 1024
 
-PIECES = (0, 1, 2, 2, 2, 2, 3, 3, 3, 3, 1, 1, 1, 0, 0, 0)
-CHUNKS = (0, 0, 0, 1, 2, 3, 0, 1, 2, 3, 1, 2, 3, 1, 2, 3)
+def piece_of(i):
+    return jnp.where(i < 2, i, jnp.where(i < 10, 2 + lax.div(i - 2, 4), 1 - lax.div(i - 10, 3)))
+
+
+def chunk_of(i):
+    return jnp.where(i < 2, 0, jnp.where(i < 10, lax.rem(i - 2, 4), 1 + lax.rem(i - 10, 3)))
 
 
 def dot_nt(a, b):
@@ -45,13 +49,6 @@
 
 def iota(shape, axis):
     return lax.broadcasted_iota(jnp.int32, shape, axis)
-
-
-def lookup(table, index):
-    value = jnp.int32(table[0])
-    for at, entry in enumerate(table[1:], 1):
-        value = jnp.where(index == at, jnp.int32(entry), value)
-    return value
 
 
 def to_row(column):
@@ -526,7 +523,7 @@
     ones = jnp.ones((KEYS, HD), BF16)
 
     def scores_of(at, b, held, peak):
-        p, yc = lookup(PIECES, at), turned(lookup(CHUNKS, at))
+        p, yc = piece_of(at), turned(chunk_of(at))
         zq = near(p)
         late = (y * RING + zq) * SPAN - (yc * RING + z) * SPAN
         shape = (SPAN, SPAN)
@@ -545,7 +542,7 @@
         peak[...] = jnp.broadcast_to(jnp.max(highest, axis=1, keepdims=True), (BLOCK, HD))
 
     def weigh(at, b, held, peak):
-        p, yc = lookup(PIECES, at), turned(lookup(CHUNKS, at))
+        p, yc = piece_of(at), turned(chunk_of(at))
         rows = slice(b * BLOCK, (b + 1) * BLOCK)
         before = s.top[p, rows, :]
         after = jnp.maximum(before, peak[...])
@@ -658,7 +655,7 @@
         prepare(i + 1)
         scores_of(jnp.minimum(i + 1, 15), 0, s.ts0, s.mx0)
         weigh(i, 1, s.ts1, s.mx1)
-        p, k = lookup(PIECES, i), lookup(CHUNKS, i)
+        p, k = piece_of(i), chunk_of(i)
 
         @pl.when((k == 3) & (p > 0))
         def _():
@@ -666,7 +663,7 @@
 
         return carry
 
-    scores_of(0, 0, s.ts0, s.mx0)
+    scores_of(jnp.int32(0), 0, s.ts0, s.mx0)
     lax.fori_loop(0, 16, step, 0)
     for p in (1, 2, 3):
         arrived(s.orb.at[p], s.opr.at[p])

time: 72.5 us -> 72.4 us (level)
  no operation moved by 1% of the time
where the time goes in v10:
time: 72.4 us; the launch traced here: 72.3 us
  Pallas kernels  69 us (95%)
  between operations  1.93 us (3%)
  local copies, waits for them, and re-layouts  1.36 us (2%)
    pallas_call x1, Pallas kernels, shards(): pl.pallas_call(kernel, out_shape=(jax.ShapeDtypeStruct((SPAN, GQ * HD), B...  69 us

profile of v10, /device:TPU:16, one launch (start us, length us, event | category | flops | bytes accessed | tf_op | source)
XLA Modules:
  0.0 72.3 jit_solution(5709205802554550586)
XLA Ops:
  1.9 69.0 %shard_map.113 = (bf16[128,1024]{1,0:T(8,128)(2,1)S(1)}, bf16[32,4,512]{2,1,0:T(4,128)(2,1)S(1)}) custom-call(s32[1]{0:T(128)S(6)} %copy.14.plen, s32[1]{0:T(128)S(6)} %copy.15.prow, s32[1,16]{1,0:T(1,128)} %clen_in.1, bf16[128,1024]{1,0:T(8,128)(2,1)} %bitcast.12, bf16[2,128,128]{2,1,0:T(8,128)(2,1)} %bitcast.14, bf16[2,896,128]{2,1,0:T(8,128)(2,1)} %bitcast.11, ...), custom_call_target="tpu_custom_call" | custom-call | flops 11000000512 | bytes 8000000 | tf_op jit(solution)/shard_map/pallas_call | solution.py:712
  70.9 0.7 copy.16
  71.6 0.7 copy.17

commit v11 on v10

--- a/solution.py
+++ b/solution.py
@@ -83,8 +83,9 @@
     "qb": pltpu.VMEM((RING, GQ * SPAN, HD), BF16),
     "ts0": pltpu.VMEM((BLOCK, KEYS), F32),
     "ts1": pltpu.VMEM((BLOCK, KEYS), F32),
-    "mx0": pltpu.VMEM((BLOCK, HD), F32),
-    "mx1": pltpu.VMEM((BLOCK, HD), F32),
+    "kp": pltpu.VMEM((BLOCK, HD), F32),
+    "pk": pltpu.VMEM((BLOCK, KEYS), BF16),
+    "ahead": pltpu.VMEM((SPAN, SPAN), F32),
     "dq": pltpu.VMEM((ROWS, STEPS, GQ * HD), BF16),
     "nkv": pltpu.VMEM((2, ROWS, STEPS, HD), BF16),
     "acc": pltpu.VMEM((RING, GQ * SPAN, HD), F32),
@@ -518,42 +519,37 @@
             s.xo[j] = total.astype(BF16)
             xi_copy(j).start()
 
-    count = BLOCK // SPAN
     first_lane = jnp.where(iota((BLOCK, HD), 1) == 0, 1.0, 0.0).astype(BF16)
     ones = jnp.ones((KEYS, HD), BF16)
 
-    def scores_of(at, b, held, peak):
+    def scores_of(at, b, held):
         p, yc = piece_of(at), turned(chunk_of(at))
-        zq = near(p)
-        late = (y * RING + zq) * SPAN - (yc * RING + z) * SPAN
+        queries = jnp.concatenate([s.qb[near(p), b * BLOCK : (b + 1) * BLOCK, :], first_lane], axis=1)
+        held[...] = dot_nn(queries, s.kb[yc])
+
+    def weigh(at, b, held):
+        p, yc = piece_of(at), turned(chunk_of(at))
+        late = (y * RING + near(p)) * SPAN - (yc * RING + z) * SPAN
         shape = (SPAN, SPAN)
-        ahead = jnp.where(iota(shape, 1) - iota(shape, 0) <= late, 0.0, MASKED)
-        ahead = jnp.concatenate([ahead] * count, axis=0)
-        queries = jnp.concatenate([s.qb[zq, b * BLOCK : (b + 1) * BLOCK, :], first_lane], axis=1)
-        scores = dot_nn(queries, s.kb[yc])
-        highest = None
-        for k in range(KEYS // HD):
-            cols = slice(k * HD, (k + 1) * HD)
-            part = scores[:, cols] * SCALE
-            if k == PRE // HD:
-                part = part + ahead
-            held[:, cols] = part
-            highest = part if highest is None else jnp.maximum(highest, part)
-        peak[...] = jnp.broadcast_to(jnp.max(highest, axis=1, keepdims=True), (BLOCK, HD))
-
-    def weigh(at, b, held, peak):
-        p, yc = piece_of(at), turned(chunk_of(at))
+        s.ahead[...] = jnp.where(iota(shape, 1) - iota(shape, 0) <= late, 0.0, MASKED)
+        for i in range(0, BLOCK, 32):
+            mine = slice(i, i + 32)
+            rows = slice(b * BLOCK + i, b * BLOCK + i + 32)
+            tiles = [held[mine, k * HD : (k + 1) * HD] for k in range(KEYS // HD)]
+            tiles[-1] = tiles[-1] + s.ahead[i % SPAN : i % SPAN + 32, :]
+            highest = tiles[0]
+            for part in tiles[1:]:
+                highest = jnp.maximum(highest, part)
+            before = s.top[p, rows, :]
+            after = jnp.maximum(before, jnp.max(highest, axis=1, keepdims=True))
+            s.top[p, rows, :] = after
+            s.kp[mine, :] = jnp.exp2((before - after) * SCALE)
+            for k, part in enumerate(tiles):
+                s.pk[mine, k * HD : (k + 1) * HD] = jnp.exp2((part - after) * SCALE).astype(BF16)
         rows = slice(b * BLOCK, (b + 1) * BLOCK)
-        before = s.top[p, rows, :]
-        after = jnp.maximum(before, peak[...])
-        keep = jnp.exp2(before - after)
-        packed = []
-        for k in range(KEYS // HD):
-            packed.append(jnp.exp2(held[:, k * HD : (k + 1) * HD] - after).astype(BF16))
-        mixed = dot_nn(jnp.concatenate(packed, axis=1), jnp.concatenate([s.vb[yc], ones], axis=1))
-        s.top[p, rows, :] = after
-        s.tot[p, rows, :] = s.tot[p, rows, :] * keep + mixed[:, HD:]
-        s.acc[p, rows, :] = s.acc[p, rows, :] * keep + mixed[:, :HD]
+        mixed = dot_nn(s.pk[...], jnp.concatenate([s.vb[yc], ones], axis=1))
+        s.tot[p, rows, :] = s.tot[p, rows, :] * s.kp[...] + mixed[:, HD:]
+        s.acc[p, rows, :] = s.acc[p, rows, :] * s.kp[...] + mixed[:, :HD]
 
     def o_copies(p):
         return [
@@ -574,7 +570,7 @@
             rows = pl.ds(pl.multiple_of(h * SPAN, SPAN), SPAN)
             total = s.tot[p, rows, :]
             s.os[p, h] = (s.acc[p, rows, :] / total).astype(BF16)
-            s.ls[p, pl.ds(h, 1), :] = to_row(s.top[p, rows, :] + log2(total))
+            s.ls[p, pl.ds(h, 1), :] = to_row(s.top[p, rows, :] * SCALE + log2(total))
 
         each_head(one)
         for copy in o_copies(p):
@@ -584,10 +580,11 @@
         def one(h):
             rows = pl.ds(pl.multiple_of(h * SPAN, SPAN), SPAN)
             levels = [to_column(s.lrb[p, pl.ds(h, 1), :], SPAN) for p in (1, 2, 3)]
-            top = s.top[0, rows, :]
+            own = s.top[0, rows, :] * SCALE
+            top = own
             for level in levels:
                 top = jnp.maximum(top, level)
-            weight = jnp.exp2(s.top[0, rows, :] - top)
+            weight = jnp.exp2(own - top)
             total = s.tot[0, rows, :] * weight
             mixed = s.acc[0, rows, :] * weight
             for p, level in zip((1, 2, 3), levels):
@@ -650,11 +647,11 @@
             project(jnp.maximum(i - 11, 0))
 
     def step(i, carry):
-        scores_of(i, 1, s.ts1, s.mx1)
-        weigh(i, 0, s.ts0, s.mx0)
+        scores_of(i, 1, s.ts1)
+        weigh(i, 0, s.ts0)
         prepare(i + 1)
-        scores_of(jnp.minimum(i + 1, 15), 0, s.ts0, s.mx0)
-        weigh(i, 1, s.ts1, s.mx1)
+        scores_of(jnp.minimum(i + 1, 15), 0, s.ts0)
+        weigh(i, 1, s.ts1)
         p, k = piece_of(i), chunk_of(i)
 
         @pl.when((k == 3) & (p > 0))
@@ -663,7 +660,7 @@
 
         return carry
 
-    scores_of(jnp.int32(0), 0, s.ts0, s.mx0)
+    scores_of(jnp.int32(0), 0, s.ts0)
     lax.fori_loop(0, 16, step, 0)
     for p in (1, 2, 3):
         arrived(s.orb.at[p], s.opr.at[p])

time: 72.4 us -> 72.6 us (level)
  no operation moved by 1% of the time
where the time goes in v11:
time: 72.6 us; the launch traced here: 72.5 us
  Pallas kernels  69.2 us (95%)
  between operations  1.93 us (3%)
  local copies, waits for them, and re-layouts  1.36 us (2%)
    pallas_call x1, Pallas kernels, shards(): pl.pallas_call(kernel, out_shape=(jax.ShapeDtypeStruct((SPAN, GQ * HD), B...  69.2 us

profile of v11, /device:TPU:16, one launch (start us, length us, event | category | flops | bytes accessed | tf_op | source)
XLA Modules:
  0.0 72.5 jit_solution(6883890160784756980)
XLA Ops:
  1.9 69.2 %shard_map.113 = (bf16[128,1024]{1,0:T(8,128)(2,1)S(1)}, bf16[32,4,512]{2,1,0:T(4,128)(2,1)S(1)}) custom-call(s32[1]{0:T(128)S(6)} %copy.14.plen, s32[1]{0:T(128)S(6)} %copy.15.prow, s32[1,16]{1,0:T(1,128)} %clen_in.1, bf16[128,1024]{1,0:T(8,128)(2,1)} %bitcast.12, bf16[2,128,128]{2,1,0:T(8,128)(2,1)} %bitcast.14, bf16[2,896,128]{2,1,0:T(8,128)(2,1)} %bitcast.11, ...), custom_call_target="tpu_custom_call" | custom-call | flops 11000000512 | bytes 8000000 | tf_op jit(solution)/shard_map/pallas_call | solution.py:709
  71.1 0.7 copy.16
  71.8 0.7 copy.17
